TPU v7x, 128 devices: a whole 4x4x4 slice. The times are simulated.
128 devices in a mesh: pre: 8 (over x, core), row: 16 (over z, y).
Axes of the slice: x: 4, y: 4, z: 4, core: 2. Of those that a mesh axis runs over, the one named last changes fastest.
Arguments:
- queries: bfloat16 [1024, 12288], P(('pre', 'row')), may hold values from -9 to 9
- prompt_ids: int32 [1024, 1], P(('pre', 'row')), may hold values from 0 to 7; in each aligned block of 8 rows (0 to 7, 8 to 15, ...) at most 2 rows name the same one
- suffix_len: int32 [1024], P(('pre', 'row')), may hold values from 1 to 256, as said below
- page_table: int32 [1024, 16], P(('pre', 'row')), may hold values from 0 to 127, as said below
- suffix_pool: bfloat16 [16384, 16, 2048], P(('pre', 'row')), may hold values from -24 to 24
- prefix_kv: bfloat16 [8, 16384, 2048], P('pre', 'row'), may hold values from -18 to 18
Outputs:
- attention: bfloat16 [1024, 12288], P(('pre', 'row'))
Inputs may be any that keep to these rules, and one draw needn't show every extreme that they name: `suffix_len`: each device's 8 rows include one of length 256. `page_table`: the rows of one device name each of that device's 128 pages exactly once. `prompt_ids`: in the rows of one device no prompt is named by more than 2 rows.
All inputs are finite; a program needn't handle non-finite values.
Results may differ from a plain program's by a relative error of at most 0.014.
Values may be sent and summed in bfloat16 or wider, within the bound.
No kernel may reach another device: no remote copies, remote signals or barrier semaphores. Data moves between devices by JAX's collectives and lax.ppermute only.
A program may use at most 512 MiB of HBM per device.

v0:
```python
import functools
import math

import jax
import jax.numpy as jnp
from jax import lax
from jax.experimental import pallas as pl
from jax.experimental.pallas import tpu as pltpu
from jax.sharding import PartitionSpec as P

KVH = 8
HD = 128
CAP = 2
GROUP = 12
ROWS = 8
WIDE = GROUP * HD
KVW = KVH * HD
NX, NC, NZ, NY = 4, 2, 4, 4
DEVS = NX * NC * NZ * NY
BLOCK = 1024
PAGE = 16
MAXP = 16
SPAN = PAGE * MAXP
SLOTS = 2 * CAP
HALVES = 2
PER_HALF = GROUP // HALVES
PAIRS = PER_HALF // 2
PART = PER_HALF * HD
LINES = HALVES * SLOTS
ARR = DEVS * LINES
HALF = DEVS * CAP
TILE = 128
UNROLL = 3
EMPTY = 256.0
SCALE = 1.0 / math.sqrt(HD)
FACTOR = SCALE / math.log(2.0)
LEAST = 1e-26
MOST = 1e30
AXES = ("pre", "row")
MB = 1 << 20
F32 = jnp.float32
BF16 = jnp.bfloat16


def dot(a, b):
    return jnp.dot(a, b, preferred_element_type=F32)


def dot_t(a, b):
    return lax.dot_general(a, b, (((1,), (1,)), ((), ())), preferred_element_type=F32)


def iota(shape, dim):
    return lax.broadcasted_iota(jnp.int32, shape, dim)


def device_number(x, c, z, y):
    return ((x * NC + c) * NZ + z) * NY + y


def routes(k, cross):
    pairs = []
    for x in range(NX):
        for c in range(NC):
            for z in range(NZ):
                for y in range(NY):
                    if (c ^ cross) == 0:
                        to = device_number(x, 0, (z + k) % NZ, y)
                    else:
                        to = device_number(x, 1, z, (y + k) % NY)
                    pairs.append((device_number(x, c, z, y), to))
    return pairs


def split_heads_kernel(head_ref, kv_ref, *refs):
    outs, (held, sems) = refs[:-2], refs[-2:]
    inward, outward = [], []
    for i, out in enumerate(outs):
        for part in range(2):
            start = pl.multiple_of(part * KVW + head_ref[i] * HD, HD)
            inward.append(
                pltpu.make_async_copy(
                    kv_ref.at[0, :, pl.ds(start, HD)], held.at[i, part], sems.at[0, i, part]
                )
            )
            outward.append(
                pltpu.make_async_copy(held.at[i, part], out.at[part], sems.at[1, i, part])
            )
    for copy in inward:
        copy.start()
    for copy, onward in zip(inward, outward):
        copy.wait()
        onward.start()
    for copy in outward:
        copy.wait()


def split_heads(heads, prefix_kv):
    n = heads.shape[0]
    return pl.pallas_call(
        split_heads_kernel,
        out_shape=[jax.ShapeDtypeStruct((2, BLOCK, HD), BF16)] * n,
        in_specs=[pl.BlockSpec(memory_space=pltpu.SMEM), pl.BlockSpec(memory_space=pltpu.HBM)],
        out_specs=[pl.BlockSpec(memory_space=pltpu.HBM)] * n,
        scratch_shapes=[
            pltpu.VMEM((n, 2, BLOCK, HD), BF16),
            pltpu.SemaphoreType.DMA((2, n, 2)),
        ],
        compiler_params=pltpu.CompilerParams(vmem_limit_bytes=8 * MB),
        name="split_heads",
    )(heads, prefix_kv)


def send_kernel(prompt_ref, q_ref, out_ref):
    wide = HALVES * NY * ROWS
    lane = iota((1, wide), 1) % ROWS
    slot = jnp.zeros((1, wide), jnp.int32)
    for i in range(ROWS):
        rank = sum((prompt_ref[j] == prompt_ref[i]).astype(jnp.int32) for j in range(i))
        slot = jnp.where(lane == i, prompt_ref[i] * CAP + rank, slot)
    unit = NY * LINES
    rows = NX * unit
    r = iota((rows, wide), 0)
    lane = iota((rows, wide), 1)
    base = r // unit * SLOTS
    half_fits = r // SLOTS % HALVES == lane // ROWS % HALVES
    first = (base + r % SLOTS == slot) & half_fits & (lane < HALVES * ROWS)
    second = (
        (base + (r + CAP) % SLOTS == slot)
        & half_fits
        & (r // LINES % NY == lane // (HALVES * ROWS))
    )
    first = first.astype(F32)
    second = second.astype(F32)
    empty_first = (1.0 - jnp.sum(first, axis=1, keepdims=True)) * EMPTY
    empty_second = (1.0 - jnp.sum(second, axis=1, keepdims=True)) * EMPTY
    first = first[:, : HALVES * ROWS].astype(BF16)
    second = second.astype(BF16)

    def stacked(heads):
        return jnp.concatenate(
            [
                q_ref[:, h * WIDE + half * PART : h * WIDE + (half + 1) * PART].astype(F32)
                for h in heads
                for half in range(HALVES)
            ],
            axis=0,
        ).astype(BF16)

    for z in range(NZ):
        piece = (dot(first, stacked([z])) + empty_first).astype(BF16)
        for x in range(NX):
            at = device_number(x, 0, z, 0) * LINES
            out_ref[at : at + unit, :] = piece[x * unit : (x + 1) * unit]
    piece = dot(second, stacked([NZ + y for y in range(NY)])) + empty_second
    piece = piece.astype(BF16)
    for x in range(NX):
        for z in range(NZ):
            at = device_number(x, 1, z, 0) * LINES
            out_ref[at : at + unit, :] = piece[x * unit : (x + 1) * unit]


def fill_sends(prompt_ids, queries):
    return pl.pallas_call(
        send_kernel,
        out_shape=jax.ShapeDtypeStruct((ARR, PART), BF16),
        in_specs=[
            pl.BlockSpec(memory_space=pltpu.SMEM),
            pl.BlockSpec(memory_space=pltpu.VMEM),
        ],
        compiler_params=pltpu.CompilerParams(vmem_limit_bytes=60 * MB),
        name="fill_sends",
    )(prompt_ids[:, 0], queries)


def suffix_kernel(table_ref, len_ref, q_ref, pool_ref, out_ref, lse_ref, kv, sems):
    for row in range(ROWS):
        for p in range(MAXP):
            pltpu.make_async_copy(
                pool_ref.at[table_ref[row, p]],
                kv.at[row, pl.ds(p * PAGE, PAGE), :],
                sems.at[row],
            ).start()

    def one(row, carry):
        pltpu.make_async_copy(kv.at[row], kv.at[row], sems.at[row]).wait()
        scores = jnp.concatenate(
            [
                dot_t(q_ref[row, h], kv[row, :, h * HD : (h + 1) * HD])
                for h in range(KVH)
            ],
            axis=0,
        )
        in_range = iota((KVH * 16, SPAN), 1) < len_ref[row]
        scores = jnp.where(in_range, scores * SCALE, -1e30)
        top = jnp.max(scores, axis=1, keepdims=True)
        weights = jnp.where(in_range, jnp.exp(scores - top), 0.0)
        total = jnp.sum(weights, axis=1, keepdims=True)
        scale = 1.0 / total
        lse = top + jnp.log(total)
        weights = weights.astype(BF16)
        for h in range(KVH):
            cut = slice(h * 16, (h + 1) * 16)
            values = kv[row, :, KVW + h * HD : KVW + (h + 1) * HD]
            out_ref[row, h] = dot(weights[cut], values) * scale[cut]
            lse_ref[row, h] = jnp.broadcast_to(lse[cut], (16, HD))
        return carry

    lax.fori_loop(0, ROWS, one, 0)


def suffix(page_table, suffix_len, queries, suffix_pool):
    q = queries.reshape(ROWS, KVH, GROUP, HD)
    q = jnp.pad(q, ((0, 0), (0, 0), (0, 16 - GROUP), (0, 0)))
    smem = pl.BlockSpec(memory_space=pltpu.SMEM)
    vmem = pl.BlockSpec(memory_space=pltpu.VMEM)
    shape = jax.ShapeDtypeStruct((ROWS, KVH, 16, HD), F32)
    out, lse = pl.pallas_call(
        suffix_kernel,
        out_shape=[shape, shape],
        in_specs=[smem, smem, vmem, pl.BlockSpec(memory_space=pl.ANY)],
        out_specs=[vmem, vmem],
        scratch_shapes=[
            pltpu.VMEM((ROWS, SPAN, 2 * KVW), BF16),
            pltpu.SemaphoreType.DMA((ROWS,)),
        ],
        compiler_params=pltpu.CompilerParams(vmem_limit_bytes=56 * MB),
        cost_estimate=pl.CostEstimate(
            flops=10**9, bytes_accessed=9 * MB, transcendentals=0
        ),
        name="suffix",
    )(page_table, suffix_len, q, suffix_pool)
    return (
        out[:, :, :GROUP].reshape(ROWS, KVH * WIDE),
        lse[:, :, :GROUP].reshape(ROWS, KVH * WIDE),
    )


def line_turn(line):
    return line // CAP % 2


def line_half(line):
    return line // SLOTS % HALVES


def gather_kernel(x_ref, q_ref, place_ref):
    pick = (iota((8, HD), 1) == 0).astype(BF16)
    held = dot_t(pick, x_ref[:, :HD]) < EMPTY / 2
    a, b = iota((ARR, ARR), 0), iota((ARR, ARR), 1)
    before = (a <= b) & (((a ^ b) & (LINES - CAP)) == 0)
    place = dot(held.astype(BF16), before.astype(BF16)).astype(jnp.int32) - 1
    place = jnp.where(held, place, -1)
    place_ref[...] = place
    line = iota((1, ARR), 1)
    for turn in range(2):
        for half in range(HALVES):
            mine = (line_turn(line) == turn) & (line_half(line) == half)
            row = jnp.where(mine, place[0:1], -1)
            gather = (row == iota((HALF, ARR), 0)).astype(BF16)
            for p in range(PAIRS):
                two = dot(gather, x_ref[:, p * 2 * HD : (p + 1) * 2 * HD]).astype(BF16)
                q_ref[turn, half * PER_HALF + 2 * p] = two[:, :HD]
                q_ref[turn, half * PER_HALF + 2 * p + 1] = two[:, HD:]


def gather_rows(arrived):
    return pl.pallas_call(
        gather_kernel,
        out_shape=[
            jax.ShapeDtypeStruct((2, GROUP, HALF, HD), BF16),
            jax.ShapeDtypeStruct((8, ARR), jnp.int32),
        ],
        compiler_params=pltpu.CompilerParams(vmem_limit_bytes=16 * MB),
        name="gather_rows",
    )(arrived)


def row_counts(place_ref):
    line = iota((1, ARR), 1)
    return [
        jnp.max(jnp.where(line_turn(line) == turn, place_ref[0:1], -1)) + 1
        for turn in range(2)
    ]


def widen(pair, column):
    lane = iota((TILE, HD), 1)
    wide = jnp.zeros((TILE, HD), F32)
    for i in range(2):
        mine = (lane % GROUP == 2 * pair + i) & (lane < 3 * GROUP)
        wide = wide + jnp.where(mine, column[i * TILE : (i + 1) * TILE], 0.0)
    return wide


def pair_rows(q_ref, turn, pair, at):
    return q_ref[turn, pl.ds(2 * pair, 2), pl.ds(at, TILE), :].reshape(2 * TILE, HD)


def plain_part(q, keys, values):
    weights = jnp.exp2(dot_t(q, keys) * FACTOR)
    cuts = [weights[:, c : c + HD] for c in range(0, weights.shape[1], HD)]
    total = jnp.sum(functools.reduce(jnp.add, cuts), axis=1, keepdims=True)
    return dot(weights.astype(BF16), values), total


def load_blocks(kv_refs, ks, vs, sems):
    copies = []
    for n, ref in enumerate(kv_refs):
        rows = pl.ds(n // 2 * BLOCK, BLOCK)
        copies.append(pltpu.make_async_copy(ref.at[0], ks.at[n % 2, rows], sems.at[n, 0]))
        copies.append(pltpu.make_async_copy(ref.at[1], vs.at[n % 2, rows], sems.at[n, 1]))
    for copy in copies:
        copy.start()
    return copies


def over_tiles(place_ref, step):
    first, second = [(count + TILE - 1) // TILE for count in row_counts(place_ref)]

    def tile(t, carry):
        turn = (t >= first).astype(jnp.int32)
        step(turn, pl.multiple_of((t - turn * first) * TILE, TILE))
        return carry

    lax.fori_loop(0, first + second, tile, 0)


def sums_kernel(blocks, first, q_ref, place_ref, *refs):
    kv_refs, refs = refs[: 2 * blocks], refs[2 * blocks :]
    out_ref, total_ref, ks, vs, sems = refs[-5:]
    for copy in load_blocks(kv_refs, ks, vs, sems):
        copy.wait()

    def step(turn, at):
        def one(pair, wide):
            q = pair_rows(q_ref, turn, pair, at)
            out, total = plain_part(q, ks[turn], vs[turn])
            out = out.reshape(2, TILE, HD)
            place = (turn, pl.ds(2 * pair, 2), pl.ds(at, TILE))
            if not first:
                out = out + refs[0][place]
            out_ref[place] = out
            return wide + widen(pair, total)

        if first:
            wide = jnp.zeros((TILE, HD), F32)
        else:
            wide = refs[1][turn, pl.ds(at, TILE), :]
        total_ref[turn, pl.ds(at, TILE), :] = lax.fori_loop(
            0, GROUP // 2, one, wide, unroll=UNROLL
        )

    over_tiles(place_ref, step)


def block_scratch(blocks):
    return [
        pltpu.VMEM((2, blocks * BLOCK, HD), BF16),
        pltpu.VMEM((2, blocks * BLOCK, HD), BF16),
        pltpu.SemaphoreType.DMA((2 * blocks, 2)),
    ]


def add_sums(rows, place, kv, state):
    blocks = len(kv) // 2
    vmem = pl.BlockSpec(memory_space=pltpu.VMEM)
    return pl.pallas_call(
        functools.partial(sums_kernel, blocks, not state),
        out_shape=[
            jax.ShapeDtypeStruct((2, GROUP, HALF, HD), F32),
            jax.ShapeDtypeStruct((2, HALF, HD), F32),
        ],
        in_specs=[vmem] * 2 + [pl.BlockSpec(memory_space=pl.ANY)] * len(kv) + [vmem] * len(state),
        out_specs=[vmem, vmem],
        scratch_shapes=block_scratch(blocks),
        compiler_params=pltpu.CompilerParams(vmem_limit_bytes=24 * MB),
        cost_estimate=pl.CostEstimate(
            flops=blocks * 4 * 10**9, bytes_accessed=8 * MB, transcendentals=0
        ),
        name="sums_%d" % blocks,
    )(rows, place, *kv, *state)


def last_kernel(q_ref, place_ref, sum_ref, total_ref, *refs):
    kv_refs, all_refs, (out_ref, os, ls, ks, vs, sems, held, held_sem) = (
        refs[:2],
        refs[2:10],
        refs[10:],
    )
    copies = load_blocks(kv_refs, ks, vs, sems)
    os[...] = jnp.zeros((2, GROUP // 2, HALF, 2 * HD), BF16)
    ls[...] = jnp.zeros((2, HALF, HD), BF16)
    for copy in copies:
        copy.wait()
    lane = iota((TILE, HD), 1)

    def keep(turn, pair, at, out, totals):
        for i in range(2):
            os[turn, pair, pl.ds(at, TILE), i * HD : (i + 1) * HD] = (
                out[i * TILE : (i + 1) * TILE] / totals[i]
            ).astype(BF16)

    def keep_lse(turn, at, total, shift):
        lse = jnp.where(lane < 3 * GROUP, shift + jnp.log(total), 0.0)
        one = lse.astype(BF16).astype(F32)
        two = (lse - one).astype(BF16).astype(F32)
        three = lse - one - two
        split = jnp.where(lane < GROUP, one, jnp.where(lane < 2 * GROUP, two, three))
        ls[turn, pl.ds(at, TILE), :] = split.astype(BF16)

    def fetch(k, turn):
        for n, ref in enumerate(all_refs):

            @pl.when(2 * k + turn == n)
            def _(ref=ref):
                copy = pltpu.make_async_copy(ref, held, held_sem.at[0])
                copy.start()
                copy.wait()

    def step(turn, at):
        before = total_ref[turn, pl.ds(at, TILE), :]

        def one(pair, wide):
            q = pair_rows(q_ref, turn, pair, at)
            out, total = plain_part(q, ks[turn], vs[turn])
            out = out + sum_ref[turn, pl.ds(2 * pair, 2), pl.ds(at, TILE), :].reshape(
                2 * TILE, HD
            )
            totals = [
                total[i * TILE : (i + 1) * TILE]
                + jnp.sum(
                    jnp.where(lane == 2 * pair + i, before, 0.0), axis=1, keepdims=True
                )
                for i in range(2)
            ]
            keep(turn, pair, at, out, totals)
            return wide + widen(pair, total)

        total = lax.fori_loop(0, GROUP // 2, one, before, unroll=UNROLL)
        keep_lse(turn, at, total, 0.0)
        known = jnp.where(lane < 3 * GROUP, total, 1.0)
        plain = (jnp.min(known) > LEAST) & (jnp.max(known) < MOST)

        @pl.when(jnp.logical_not(plain))
        def _():
            def again(pair, carry):
                q = pair_rows(q_ref, turn, pair, at)

                def block(k, state):
                    top, amount, acc = state
                    fetch(k, turn)
                    score = dot_t(q, held[0])
                    high = jnp.maximum(top, jnp.max(score, axis=1, keepdims=True))
                    weights = jnp.exp2(score * FACTOR - high * FACTOR)
                    fade = jnp.exp2((top - high) * FACTOR)
                    amount = amount * fade + jnp.sum(weights, axis=1, keepdims=True)
                    return high, amount, acc * fade + dot(weights.astype(BF16), held[1])

                top, amount, acc = lax.fori_loop(
                    0,
                    4,
                    block,
                    (
                        jnp.full((2 * TILE, 1), -1e30, F32),
                        jnp.zeros((2 * TILE, 1), F32),
                        jnp.zeros((2 * TILE, HD), F32),
                    ),
                )
                keep(turn, pair, at, acc, [amount[:TILE], amount[TILE:]])
                return carry[0] + widen(pair, amount), carry[1] + widen(pair, top * SCALE)

            empty = jnp.zeros((TILE, HD), F32)
            amount, shift = lax.fori_loop(0, GROUP // 2, again, (empty, empty))
            keep_lse(turn, at, amount, shift)

    over_tiles(place_ref, step)

    place_col = jnp.transpose(place_ref[...].astype(F32))[:, 0:1].astype(jnp.int32)
    line = iota((ARR, 1), 0)
    scatter = jnp.concatenate(
        [
            (
                jnp.where((line_turn(line) == turn) & (line_half(line) == half), place_col, -1)
                == iota((ARR, HALF), 1)
            ).astype(BF16)
            for turn in range(2)
            for half in range(HALVES)
        ],
        axis=1,
    )
    for p in range(PAIRS):
        source = jnp.concatenate(
            [os[turn, half * PAIRS + p] for turn in range(2) for half in range(HALVES)], axis=0
        )
        out_ref[:, p * 2 * HD : (p + 1) * 2 * HD] = dot(scatter, source).astype(BF16)
    source = jnp.concatenate([ls[0], ls[0], ls[1], ls[1]], axis=0)
    out_ref[:, PART:] = dot(scatter, source).astype(BF16)


def finish_prefix(rows, place, state, last, everything):
    vmem = pl.BlockSpec(memory_space=pltpu.VMEM)
    return pl.pallas_call(
        last_kernel,
        out_shape=jax.ShapeDtypeStruct((ARR, PART + HD), BF16),
        in_specs=[vmem] * 4 + [pl.BlockSpec(memory_space=pl.ANY)] * 10,
        scratch_shapes=[
            pltpu.VMEM((2, GROUP // 2, HALF, 2 * HD), BF16),
            pltpu.VMEM((2, HALF, HD), BF16),
            *block_scratch(1),
            pltpu.VMEM((2, BLOCK, HD), BF16),
            pltpu.SemaphoreType.DMA((1,)),
        ],
        compiler_params=pltpu.CompilerParams(vmem_limit_bytes=32 * MB),
        cost_estimate=pl.CostEstimate(
            flops=6 * 10**9, bytes_accessed=8 * MB, transcendentals=0
        ),
        name="finish_prefix",
    )(rows, place, *state, *last, *everything)


def merge_kernel(at_ref, back_ref, so_ref, sl_ref, out_ref):
    picked = KVH * 4 * ROWS
    line = iota((picked, ARR), 1)
    first = dot((at_ref[...] == line).astype(BF16), back_ref[...])
    second = dot((at_ref[...] + SLOTS == line).astype(BF16), back_ref[:, :PART])
    spread = (
        (iota((HD, WIDE), 0) % GROUP == iota((HD, WIDE), 1) // HD)
        & (iota((HD, WIDE), 0) < 3 * GROUP)
    ).astype(BF16)
    lse = dot(first[:, PART:].astype(BF16), spread)
    for h in range(KVH):
        cut = slice(h * WIDE, (h + 1) * WIDE)
        rows = [slice((h * 4 + j) * ROWS, (h * 4 + j + 1) * ROWS) for j in range(4)]
        parts = [
            (lse[r], jnp.concatenate([first[r, :PART], second[r]], axis=1)) for r in rows
        ]
        parts.append((sl_ref[:, cut], so_ref[:, cut]))
        top = functools.reduce(jnp.maximum, [p[0] for p in parts])
        weights = [jnp.exp(p[0] - top) for p in parts]
        total = functools.reduce(jnp.add, weights)
        acc = functools.reduce(jnp.add, [w * p[1] for w, p in zip(weights, parts)])
        out_ref[:, cut] = (acc / total).astype(BF16)


def merge(prompt_ids, back, so, sl):
    prompt = prompt_ids[:, 0]
    earlier = jnp.arange(ROWS)[None, :] < jnp.arange(ROWS)[:, None]
    rank = jnp.sum(((prompt[:, None] == prompt[None, :]) & earlier).astype(jnp.int32), axis=1)
    h = jnp.arange(KVH)[:, None, None]
    j = jnp.arange(4)[None, :, None]
    c = h // 4
    z = jnp.where(c == 0, h, j)
    y = jnp.where(c == 0, j, h - 4)
    place = (prompt % 2 != c).astype(jnp.int32) * CAP + rank
    at = device_number(prompt // 2, c, z, y) * LINES + place
    return pl.pallas_call(
        merge_kernel,
        out_shape=jax.ShapeDtypeStruct((ROWS, KVH * WIDE), BF16),
        compiler_params=pltpu.CompilerParams(vmem_limit_bytes=16 * MB),
        name="merge",
    )(at.reshape(-1, 1), back, so, sl)


def exchange(array):
    width = array.shape[1]
    moved = lax.all_to_all(
        array.reshape(DEVS, LINES, width), AXES, split_axis=0, concat_axis=0, tiled=True
    )
    return moved.reshape(ARR, width)


def body(queries, prompt_ids, suffix_len, page_table, suffix_pool, prefix_kv):
    c = lax.axis_index("pre") % NC
    z = lax.axis_index("row") // NY
    y = lax.axis_index("row") % NY
    heads = jnp.stack(
        [
            jnp.where(c ^ cross == 0, (z + k) % NZ, NZ + (y + k) % NY)
            for k in range(4)
            for cross in range(2)
        ]
    ).astype(jnp.int32)
    sends = fill_sends(prompt_ids, queries)
    sends, heads = lax.optimization_barrier((sends, heads))
    arrived = exchange(sends)
    pieces = split_heads(heads, prefix_kv)

    def move(n, piece):
        return lax.ppermute(piece, AXES, routes(n // 2, n % 2))

    kv = list(pieces)
    for n in (1, 2, 3, 6, 7):
        kv[n] = move(n, pieces[n])
    kv[1], later = lax.optimization_barrier((kv[1], pieces[4]))
    kv[4] = move(4, later)
    arrived, kv[1] = lax.optimization_barrier((arrived, kv[1]))
    rows, place = gather_rows(arrived)
    state = add_sums(rows, place, kv[0:2], ())
    state, kv[2], kv[3], kv[6], kv[7], later = lax.optimization_barrier(
        (state, kv[2], kv[3], kv[6], kv[7], pieces[5])
    )
    kv[5] = move(5, later)
    state = add_sums(rows, place, kv[2:4] + kv[6:8], state)
    parts = finish_prefix(rows, place, state, kv[4:6], kv)
    parts, queries = lax.optimization_barrier((parts, queries))
    so, sl = suffix(page_table, suffix_len, queries, suffix_pool)
    return merge(prompt_ids, exchange(parts), so, sl)


def solution(mesh):
    return jax.shard_map(
        body,
        mesh=mesh,
        in_specs=(
            P(("pre", "row"), None),
            P(("pre", "row"), None),
            P(("pre", "row")),
            P(("pre", "row"), None),
            P(("pre", "row"), None, None),
            P("pre", "row", None),
        ),
        out_specs=P(("pre", "row"), None),
        check_vma=False,
    )
```

profile of v0, /device:TPU:0, one launch (start us, length us, event | category | flops | bytes accessed | tf_op | source)
XLA Modules:
  0.0 218.5 jit_solution(9830488204245995408)
XLA Ops:
  0.0 2.5 %fill_sends.1 = bf16[1024,768]{1,0:T(8,128)(2,1)} custom-call(s32[8]{0:T(128)} %bitcast.27, bf16[8,12288]{1,0:T(8,128)(2,1)} %q_ref.1), custom_call_target="tpu_custom_call" | custom-call | tf_op jit(solution)/shard_map/fill_sends/pallas_call | solution.py:164
  2.5 0.1 stack.35.head_ref
  2.6 11.1 %all-to-all-start = ((bf16[128,8,768]{2,1,0:T(8,128)(2,1)}), bf16[128,8,768]{2,1,0:T(8,128)(2,1)S(1)}, u32[]{:S(2)}, u32[]{:S(2)}) async-start(bf16[128,8,768]{2,1,0:T(8,128)(2,1)} %bitcast.24), calls=%async_computation | async-start | bytes 3145728 | tf_op jit(solution)/shard_map/all_to_all | solution.py:567
  13.8 0.0 copy-start
  13.8 2.2 copy-done
  16.0 3.5 %split_heads.1 = (bf16[2,1024,128]{2,1,0:T(8,128)(2,1)S(1)}, bf16[2,1024,128]{2,1,0:T(8,128)(2,1)S(1)}, bf16[2,1024,128]{2,1,0:T(8,128)(2,1)}, bf16[2,1024,128]{...) custom-call(s32[8]{0:T(128)S(1)} %stack.35.head_ref, ...), custom_call_target="tpu_custom_call" | custom-call | tf_op jit(solution)/shard_map/split_heads/pallas_call | solution.py:100
  19.5 0.1 collective-permute-start
  19.6 1.2 collective-permute-start.1
  20.8 1.0 collective-permute-start.2
  21.8 3.5 %collective-permute-start.3 = (bf16[2,1024,128]{2,1,0:T(8,128)(2,1)}, bf16[2,1024,128]{2,1,0:T(8,128)(2,1)}, u32[]{:S(2)}, u32[]{:S(2)}) collective-permute-start(bf16[2,1024,128]{2,1,0:T(8,128)(2,1)} %get-tuple-element.50), channel_id=1, source_target_pairs={{0,12},{1,13},{2,14},{3,15},{4,0},{5,1},{6,2},{7,3},{8,4},{9,5},{1... | collective-permute-start | bytes 1572872 | tf_op jit(solution)/shard_map/ppermute | solution.py:590
  25.3 0.3 collective-permute-start.4
  25.7 1.5 collective-permute-start.5
  27.2 11.1 %all-to-all-done = bf16[128,8,768]{2,1,0:T(8,128)(2,1)S(1)} async-done(((bf16[128,8,768]{2,1,0:T(8,128)(2,1)}), bf16[128,8,768]{2,1,0:T(8,128)(2,1)S(1)}, u32[]{:S(2)}, u32[]{:S(2)}) %all-to-all-start) | async-done | bytes 1572896 | tf_op jit(solution)/shard_map/all_to_all | solution.py:567
  38.2 2.4 %gather_rows.1 = (bf16[2,12,256,128]{3,2,1,0:T(8,128)(2,1)S(1)}, s32[8,1024]{1,0:T(8,128)S(1)}) custom-call(bf16[1024,768]{1,0:T(8,128)(2,1)S(1)} %bitcast.22), custom_call_target="tpu_custom_call" | custom-call | tf_op jit(solution)/shard_map/gather_rows/pallas_call | solution.py:268
  40.7 6.3 %sums_1.1 = (f32[2,12,256,128]{3,2,1,0:T(8,128)S(1)}, f32[2,256,128]{2,1,0:T(8,128)S(1)}) custom-call(bf16[2,12,256,128]{3,2,1,0:T(8,128)(2,1)S(1)} %get-tuple-element.42.q_ref, s32[8,1024]{1,0:T(8,128)S(1)} %get-tuple-element.43.place_ref, bf16[2,1024,128]{2,1,0:T(8,128)(2,1)S(1)} %get-tuple-element.44.refs_0_.refs_2_, ...), custom_call_target="tpu_custom_call" | custom-call | flops 4000000000 | bytes 8388608 | tf_op jit(solution)/shard_map/sums_1/pallas_call | solution.py:368
  47.0 3.6 %collective-permute-start.6 = (bf16[2,1024,128]{2,1,0:T(8,128)(2,1)S(1)}, bf16[2,1024,128]{2,1,0:T(8,128)(2,1)S(1)}, u32[]{:S(2)}, u32[]{:S(2)}) collective-permute-start(bf16[2,1024,128]{2,1,0:T(8,128)(2,1)S(1)} %get-tuple-element.62), channel_id=1, source_target_pairs={{0,18},{1,19},{2,16},{3,17},{4,22},{5,23},{6,20},{7,21},{8,26},{9,... | collective-permute-start | bytes 1572872 | tf_op jit(solution)/shard_map/ppermute | solution.py:590
  50.6 12.7 %sums_2.1 = (f32[2,12,256,128]{3,2,1,0:T(8,128)S(1)}, f32[2,256,128]{2,1,0:T(8,128)S(1)}) custom-call(bf16[2,12,256,128]{3,2,1,0:T(8,128)(2,1)S(1)} %get-tuple-element.42.q_ref, s32[8,1024]{1,0:T(8,128)S(1)} %get-tuple-element.43.place_ref, bf16[2,1024,128]{2,1,0:T(8,128)(2,1)} %collective-permute-done.1.refs_0_.refs_4_, ...), custom_call_target="tpu_custom_call" | custom-call | flops 8000000000 | bytes 8388608 | tf_op jit(solution)/shard_map/sums_2/pallas_call | solution.py:368
  63.3 111.2 %finish_prefix.1 = bf16[1024,896]{1,0:T(8,128)(2,1)S(1)} custom-call(bf16[2,12,256,128]{3,2,1,0:T(8,128)(2,1)S(1)} %get-tuple-element.42.q_ref, s32[8,1024]{1,0:T(8,128)S(1)} %get-tuple-element.43.place_ref, f32[2,12,256,128]{3,2,1,0:T(8,128)S(1)} %get-tuple-element.59.sum_ref, f32[2,256,128]{2,1,0:T(8,128)S(1)} %get-tuple-element.60.total_ref, ...), custom_call_target="tpu_custom_call" | custom-call | flops 6000000000 | bytes 8388608 | tf_op jit(solution)/shard_map/finish_prefix/pallas_call | solution.py:503
  174.5 1.2 copy-done.1
  175.7 13.5 %all-to-all-start.1 = ((bf16[128,8,896]{2,1,0:T(8,128)(2,1)}), bf16[128,8,896]{2,1,0:T(8,128)(2,1)S(1)}, u32[]{:S(2)}, u32[]{:S(2)}) async-start(bf16[128,8,896]{2,1,0:T(8,128)(2,1)} %bitcast.23), calls=%async_computation.1 | async-start | bytes 3670016 | tf_op jit(solution)/shard_map/all_to_all | solution.py:567
  189.3 0.2 convert_reduce_fusion
  189.5 0.1 iota_select_fusion.1
  189.5 0.1 add_multiply_fusion
  189.6 0.1 multiply_add_fusion
  189.7 0.1 reshape.329.at_ref
  189.8 0.2 reshape.325
  190.0 0.8 pad.4.q_ref
  190.7 6.9 %suffix.1 = (f32[8,8,16,128]{3,2,1,0:T(8,128)}, f32[8,8,16,128]{3,2,1,0:T(8,128)}) custom-call(s32[8,16]{1,0:T(8,128)} %table_ref.1, s32[8]{0:T(128)} %len_ref.1, bf16[8,8,16,128]{3,2,1,0:T(8,128)(2,1)} %pad.4.q_ref, bf16[128,16,2048]{2,1,0:T(8,128)(2,1)} %pool_ref.1), custom_call_target="tpu_custom_call" | custom-call | flops 1000000000 | bytes 9437184 | tf_op jit(solution)/shard_map/suffix/pallas_call | solution.py:218
  197.7 1.1 reshape.326.so_ref
  198.8 1.1 reshape.327.sl_ref
  199.9 16.4 %all-to-all-done.1 = bf16[128,8,896]{2,1,0:T(8,128)(2,1)S(1)} async-done(((bf16[128,8,896]{2,1,0:T(8,128)(2,1)}), bf16[128,8,896]{2,1,0:T(8,128)(2,1)S(1)}, u32[]{:S(2)}, u32[]{:S(2)}) %all-to-all-start.1) | async-done | bytes 1835040 | tf_op jit(solution)/shard_map/all_to_all | solution.py:567
  216.3 2.2 %merge.1 = bf16[8,12288]{1,0:T(8,128)(2,1)} custom-call(s32[256,1]{1,0:T(8,128)S(1)} %reshape.329.at_ref, bf16[1024,896]{1,0:T(8,128)(2,1)S(1)} %bitcast.21, f32[8,12288]{1,0:T(8,128)S(1)} %reshape.326.so_ref, f32[8,12288]{1,0:T(8,128)S(1)} %reshape.327.sl_ref), custom_call_target="tpu_custom_call" | custom-call | tf_op jit(solution)/shard_map/merge/pallas_call | solution.py:557
  (15 shorter events, 0.0 us)
Async XLA Ops:
  2.6 35.6 %all-to-all-start = ((bf16[128,8,768]{2,1,0:T(8,128)(2,1)}), bf16[128,8,768]{2,1,0:T(8,128)(2,1)S(1)}, u32[]{:S(2)}, u32[]{:S(2)}) async-start(bf16[128,8,768]{2,1,0:T(8,128)(2,1)} %bitcast.24), calls=%async_computation | async-start | bytes 3145728 | tf_op jit(solution)/shard_map/all_to_all | solution.py:567
  13.8 2.2 %copy-start = (bf16[1,1024,2048]{2,1,0:T(8,128)(2,1)S(1)}, bf16[1,1024,2048]{2,1,0:T(8,128)(2,1)}, u32[]{:S(2)}) copy-start(bf16[1,1024,2048]{2,1,0:T(8,128)(2,1)} %kv_ref.1) | copy-start | bytes 12582916
  19.5 6.2 %collective-permute-start = (bf16[2,1024,128]{2,1,0:T(8,128)(2,1)S(1)}, bf16[2,1024,128]{2,1,0:T(8,128)(2,1)S(1)}, u32[]{:S(2)}, u32[]{:S(2)}) collective-permute-start(bf16[2,1024,128]{2,1,0:T(8,128)(2,1)S(1)} %get-tuple-element.38), channel_id=1, source_target_pairs={{0,16},{1,17},{2,18},{3,19},{4,20},{5,21},{6,22},{7,23},{8,24},{9,... | collective-permute-start | bytes 1572872 | tf_op jit(solution)/shard_map/ppermute | solution.py:590
  19.6 27.4 %collective-permute-start.1 = (bf16[2,1024,128]{2,1,0:T(8,128)(2,1)}, bf16[2,1024,128]{2,1,0:T(8,128)(2,1)}, u32[]{:S(2)}, u32[]{:S(2)}) collective-permute-start(bf16[2,1024,128]{2,1,0:T(8,128)(2,1)} %get-tuple-element.48), channel_id=1, source_target_pairs={{0,4},{1,5},{2,6},{3,7},{4,8},{5,9},{6,10},{7,11},{8,12},{9,13},{1... | collective-permute-start | bytes 1572872 | tf_op jit(solution)/shard_map/ppermute | solution.py:590
  20.8 26.2 %collective-permute-start.2 = (bf16[2,1024,128]{2,1,0:T(8,128)(2,1)}, bf16[2,1024,128]{2,1,0:T(8,128)(2,1)}, u32[]{:S(2)}, u32[]{:S(2)}) collective-permute-start(bf16[2,1024,128]{2,1,0:T(8,128)(2,1)} %get-tuple-element.49), channel_id=1, source_target_pairs={{0,17},{1,18},{2,19},{3,16},{4,21},{5,22},{6,23},{7,20},{8,25},{9,... | collective-permute-start | bytes 1572872 | tf_op jit(solution)/shard_map/ppermute | solution.py:590
  21.8 25.1 %collective-permute-start.3 = (bf16[2,1024,128]{2,1,0:T(8,128)(2,1)}, bf16[2,1024,128]{2,1,0:T(8,128)(2,1)}, u32[]{:S(2)}, u32[]{:S(2)}) collective-permute-start(bf16[2,1024,128]{2,1,0:T(8,128)(2,1)} %get-tuple-element.50), channel_id=1, source_target_pairs={{0,12},{1,13},{2,14},{3,15},{4,0},{5,1},{6,2},{7,3},{8,4},{9,5},{1... | collective-permute-start | bytes 1572872 | tf_op jit(solution)/shard_map/ppermute | solution.py:590
  25.3 21.7 %collective-permute-start.4 = (bf16[2,1024,128]{2,1,0:T(8,128)(2,1)}, bf16[2,1024,128]{2,1,0:T(8,128)(2,1)}, u32[]{:S(2)}, u32[]{:S(2)}) collective-permute-start(bf16[2,1024,128]{2,1,0:T(8,128)(2,1)} %get-tuple-element.51), channel_id=1, source_target_pairs={{0,19},{1,16},{2,17},{3,18},{4,23},{5,20},{6,21},{7,22},{8,27},{9,... | collective-permute-start | bytes 1572872 | tf_op jit(solution)/shard_map/ppermute | solution.py:590
  25.7 37.6 %collective-permute-start.5 = (bf16[2,1024,128]{2,1,0:T(8,128)(2,1)}, bf16[2,1024,128]{2,1,0:T(8,128)(2,1)}, u32[]{:S(2)}, u32[]{:S(2)}) collective-permute-start(bf16[2,1024,128]{2,1,0:T(8,128)(2,1)} %get-tuple-element.61), channel_id=1, source_target_pairs={{0,8},{1,9},{2,10},{3,11},{4,12},{5,13},{6,14},{7,15},{8,0},{9,1},... | collective-permute-start | bytes 1572872 | tf_op jit(solution)/shard_map/ppermute | solution.py:590
  47.0 16.3 %collective-permute-start.6 = (bf16[2,1024,128]{2,1,0:T(8,128)(2,1)S(1)}, bf16[2,1024,128]{2,1,0:T(8,128)(2,1)S(1)}, u32[]{:S(2)}, u32[]{:S(2)}) collective-permute-start(bf16[2,1024,128]{2,1,0:T(8,128)(2,1)S(1)} %get-tuple-element.62), channel_id=1, source_target_pairs={{0,18},{1,19},{2,16},{3,17},{4,22},{5,23},{6,20},{7,21},{8,26},{9,... | collective-permute-start | bytes 1572872 | tf_op jit(solution)/shard_map/ppermute | solution.py:590
  174.5 1.2 copy-start.1
  175.7 13.5 %copy-start.3 = (s32[8,1]{0,1:T(1,128)S(1)}, s32[8,1]{0,1:T(1,128)}, u32[]{:S(2)}) copy-start(s32[8,1]{0,1:T(1,128)} %param.7) | copy-start | bytes 100
  175.7 14.1 %copy-start.2 = (bf16[8,12288]{1,0:T(8,128)(2,1)S(1)}, bf16[8,12288]{1,0:T(8,128)(2,1)}, u32[]{:S(2)}) copy-start(bf16[8,12288]{1,0:T(8,128)(2,1)} %q_ref.1) | copy-start | bytes 589828
  175.7 40.6 %all-to-all-start.1 = ((bf16[128,8,896]{2,1,0:T(8,128)(2,1)}), bf16[128,8,896]{2,1,0:T(8,128)(2,1)S(1)}, u32[]{:S(2)}, u32[]{:S(2)}) async-start(bf16[128,8,896]{2,1,0:T(8,128)(2,1)} %bitcast.23), calls=%async_computation.1 | async-start | bytes 3670016 | tf_op jit(solution)/shard_map/all_to_all | solution.py:567
where the time goes:
time: 221 us; the launch traced here: 218 us
  Pallas kernels  148 us (67%)
  starting transfers between devices  35.9 us (16%)
  waiting for transfers between devices  27.5 us (12%)
  local copies, waits for them, and re-layouts  6.73 us (3%)
    pallas_call x1, Pallas kernels, finish_prefix(): pl.pallas_call(last_kernel, out_shape=jax.ShapeDtypeStruct((ARR, PART + H...  111 us
    all_to_all x2, waiting for transfers between devices, exchange(): lax.all_to_all(array.reshape(DEVS, LINES, width), AXES, split_axis=0, con...  27.5 us
    all_to_all x2, starting transfers between devices, exchange(): lax.all_to_all(array.reshape(DEVS, LINES, width), AXES, split_axis=0, con...  24.6 us
    pallas_call x2, Pallas kernels, add_sums(): pl.pallas_call(functools.partial(sums_kernel, blocks, not state), out_sha...  18.9 us
    ppermute x7, starting transfers between devices, move(): return lax.ppermute(piece, AXES, routes(n // 2, n % 2))  11.3 us
    pallas_call x1, Pallas kernels, suffix(): pl.pallas_call(suffix_kernel, out_shape=[shape, shape], in_specs=[smem, s...  6.93 us
  transfers between devices with their start and end apart: 9, of which 2 were waited for; matrix products, arithmetic and copies ran while one was open for 2% of the time, Pallas kernels for 15%

commit v1 on v0

--- a/solution.py
+++ b/solution.py
@@ -592,10 +592,10 @@
     kv = list(pieces)
     for n in (1, 2, 3, 6, 7):
         kv[n] = move(n, pieces[n])
-    kv[1], later = lax.optimization_barrier((kv[1], pieces[4]))
-    kv[4] = move(4, later)
     arrived, kv[1] = lax.optimization_barrier((arrived, kv[1]))
     rows, place = gather_rows(arrived)
+    place, later = lax.optimization_barrier((place, pieces[4]))
+    kv[4] = move(4, later)
     state = add_sums(rows, place, kv[0:2], ())
     state, kv[2], kv[3], kv[6], kv[7], later = lax.optimization_barrier(
         (state, kv[2], kv[3], kv[6], kv[7], pieces[5])

time: 221 us -> 207 us (0.937)
  Pallas kernels: 148 us -> 102 us
  starting transfers between devices: 35.9 us -> 60.4 us
  waiting for transfers between devices: 27.5 us -> 34.2 us
    pallas_call x1, Pallas kernels: 111 us -> 71 us  [finish_prefix(): pl.pallas_call(last_kernel, out_shape=jax.ShapeDtypeStruct((ARR, PART + H...]
    all_to_all x2, starting transfers between devices: 24.6 us -> 51.7 us  [exchange(): lax.all_to_all(array.reshape(DEVS, LINES, width), AXES, split_axis=0, con...]
    ppermute x7, waiting for transfers between devices: 0.02 us -> 5.74 us  [move(): return lax.ppermute(piece, AXES, routes(n // 2, n % 2))]
    pallas_call x2, Pallas kernels: 18.9 us -> 13.3 us  [add_sums(): pl.pallas_call(functools.partial(sums_kernel, blocks, not state), out_sha...]
    ppermute x7, starting transfers between devices: 11.3 us -> 8.67 us  [move(): return lax.ppermute(piece, AXES, routes(n // 2, n % 2))]
  transfers between devices with their start and end apart: 9 -> 9, of which waited for: 2 -> 5; matrix products, arithmetic and copies ran while one was open for 2% -> 2% of each run, Pallas kernels for 15% -> 13%
where the time goes in v1:
time: 207 us; the launch traced here: 205 us
  Pallas kernels  102 us (49%)
  starting transfers between devices  60.4 us (29%)
  waiting for transfers between devices  34.2 us (17%)
  local copies, waits for them, and re-layouts  7.56 us (4%)
    pallas_call x1, Pallas kernels, finish_prefix(): pl.pallas_call(last_kernel, out_shape=jax.ShapeDtypeStruct((ARR, PART + H...  71 us
    all_to_all x2, starting transfers between devices, exchange(): lax.all_to_all(array.reshape(DEVS, LINES, width), AXES, split_axis=0, con...  51.7 us
    all_to_all x2, waiting for transfers between devices, exchange(): lax.all_to_all(array.reshape(DEVS, LINES, width), AXES, split_axis=0, con...  28.4 us
    pallas_call x2, Pallas kernels, add_sums(): pl.pallas_call(functools.partial(sums_kernel, blocks, not state), out_sha...  13.3 us
    ppermute x7, starting transfers between devices, move(): return lax.ppermute(piece, AXES, routes(n // 2, n % 2))  8.67 us
    pallas_call x1, Pallas kernels, suffix(): pl.pallas_call(suffix_kernel, out_shape=[shape, shape], in_specs=[smem, s...  6.94 us
    ppermute x7, waiting for transfers between devices, move(): return lax.ppermute(piece, AXES, routes(n // 2, n % 2))  5.74 us
    unnamed x12, local copies, waits for them, and re-layouts  4.26 us
  transfers between devices with their start and end apart: 9, of which 5 were waited for; matrix products, arithmetic and copies ran while one was open for 2% of the time, Pallas kernels for 13%

profile of v1, /device:TPU:0, one launch (start us, length us, event | category | flops | bytes accessed | tf_op | source)
XLA Modules:
  0.0 204.6 jit_solution(12640400591006573008)
XLA Ops:
  0.0 2.5 %fill_sends.1 = bf16[1024,768]{1,0:T(8,128)(2,1)} custom-call(s32[8]{0:T(128)} %bitcast.27, bf16[8,12288]{1,0:T(8,128)(2,1)} %q_ref.1), custom_call_target="tpu_custom_call" | custom-call | tf_op jit(solution)/shard_map/fill_sends/pallas_call | solution.py:164
  2.5 0.1 stack.35.head_ref
  2.6 11.1 %all-to-all-start = ((bf16[128,8,768]{2,1,0:T(8,128)(2,1)}), bf16[128,8,768]{2,1,0:T(8,128)(2,1)S(1)}, u32[]{:S(2)}, u32[]{:S(2)}) async-start(bf16[128,8,768]{2,1,0:T(8,128)(2,1)} %bitcast.24), calls=%async_computation | async-start | bytes 3145728 | tf_op jit(solution)/shard_map/all_to_all | solution.py:567
  13.8 2.2 %copy-done = bf16[1,1024,2048]{2,1,0:T(8,128)(2,1)S(1)} copy-done((bf16[1,1024,2048]{2,1,0:T(8,128)(2,1)S(1)}, bf16[1,1024,2048]{2,1,0:T(8,128)(2,1)}, u32[]{:S(2)}) %copy-start) | copy-done | bytes 4194328
  16.0 3.4 %split_heads.1 = (bf16[2,1024,128]{2,1,0:T(8,128)(2,1)S(1)}, bf16[2,1024,128]{2,1,0:T(8,128)(2,1)S(1)}, bf16[2,1024,128]{2,1,0:T(8,128)(2,1)}, bf16[2,1024,128]{...) custom-call(s32[8]{0:T(128)S(1)} %stack.35.head_ref, ...), custom_call_target="tpu_custom_call" | custom-call | tf_op jit(solution)/shard_map/split_heads/pallas_call | solution.py:100
  19.3 0.8 copy-done.2
  20.1 1.2 collective-permute-start.1
  21.4 1.0 collective-permute-start.2
  22.4 3.5 %collective-permute-start.3 = (bf16[2,1024,128]{2,1,0:T(8,128)(2,1)}, bf16[2,1024,128]{2,1,0:T(8,128)(2,1)}, u32[]{:S(2)}, u32[]{:S(2)}) collective-permute-start(bf16[2,1024,128]{2,1,0:T(8,128)(2,1)} %get-tuple-element.50), channel_id=1, source_target_pairs={{0,12},{1,13},{2,14},{3,15},{4,0},{5,1},{6,2},{7,3},{8,4},{9,5},{1... | collective-permute-start | bytes 1572872 | tf_op jit(solution)/shard_map/ppermute | solution.py:590
  25.9 0.3 collective-permute-start.4
  26.2 12.0 %all-to-all-done = bf16[128,8,768]{2,1,0:T(8,128)(2,1)S(1)} async-done(((bf16[128,8,768]{2,1,0:T(8,128)(2,1)}), bf16[128,8,768]{2,1,0:T(8,128)(2,1)S(1)}, u32[]{:S(2)}, u32[]{:S(2)}) %all-to-all-start) | async-done | bytes 1572896 | tf_op jit(solution)/shard_map/all_to_all | solution.py:567
  38.2 2.4 %gather_rows.1 = (bf16[2,12,256,128]{3,2,1,0:T(8,128)(2,1)S(1)}, s32[8,1024]{1,0:T(8,128)S(1)}) custom-call(bf16[1024,768]{1,0:T(8,128)(2,1)S(1)} %bitcast.22), custom_call_target="tpu_custom_call" | custom-call | tf_op jit(solution)/shard_map/gather_rows/pallas_call | solution.py:268
  40.7 4.3 %sums_1.1 = (f32[2,12,256,128]{3,2,1,0:T(8,128)S(1)}, f32[2,256,128]{2,1,0:T(8,128)S(1)}) custom-call(bf16[2,12,256,128]{3,2,1,0:T(8,128)(2,1)S(1)} %get-tuple-element.40.q_ref, s32[8,1024]{1,0:T(8,128)S(1)} %get-tuple-element.43.place_ref, bf16[2,1024,128]{2,1,0:T(8,128)(2,1)S(1)} %get-tuple-element.44.refs_0_.refs_2_, ...), custom_call_target="tpu_custom_call" | custom-call | flops 4000000000 | bytes 8388608 | tf_op jit(solution)/shard_map/sums_1/pallas_call | solution.py:368
  45.0 1.6 collective-permute-done.1.refs_0_.refs_4_
  46.6 0.1 collective-permute-start.6
  46.7 2.5 %collective-permute-start.5 = (bf16[2,1024,128]{2,1,0:T(8,128)(2,1)S(1)}, bf16[2,1024,128]{2,1,0:T(8,128)(2,1)S(1)}, u32[]{:S(2)}, u32[]{:S(2)}) collective-permute-start(bf16[2,1024,128]{2,1,0:T(8,128)(2,1)S(1)} %get-tuple-element.61), channel_id=1, source_target_pairs={{0,8},{1,9},{2,10},{3,11},{4,12},{5,13},{6,14},{7,15},{8,0},{9,1},... | collective-permute-start | bytes 1572872 | tf_op jit(solution)/shard_map/ppermute | solution.py:590
  49.2 9.0 %sums_2.1 = (f32[2,12,256,128]{3,2,1,0:T(8,128)S(1)}, f32[2,256,128]{2,1,0:T(8,128)S(1)}) custom-call(bf16[2,12,256,128]{3,2,1,0:T(8,128)(2,1)S(1)} %get-tuple-element.40.q_ref, s32[8,1024]{1,0:T(8,128)S(1)} %get-tuple-element.43.place_ref, bf16[2,1024,128]{2,1,0:T(8,128)(2,1)} %collective-permute-done.1.refs_0_.refs_4_, ...), custom_call_target="tpu_custom_call" | custom-call | flops 8000000000 | bytes 8388608 | tf_op jit(solution)/shard_map/sums_2/pallas_call | solution.py:368
  58.3 3.5 %collective-permute-done.6.refs_1_.refs_7_ = bf16[2,1024,128]{2,1,0:T(8,128)(2,1)S(1)} collective-permute-done((bf16[2,1024,128]{2,1,0:T(8,128)(2,1)S(1)}, bf16[2,1024,128]{2,1,0:T(8,128)(2,1)S(1)}, u32[]{:S(2)}, u32[]{:S(2)}) %collective-permute-start.6) | collective-permute-done | bytes 524320 | tf_op jit(solution)/shard_map/ppermute | solution.py:590
  61.8 0.6 collective-permute-done.5.refs_0_.refs_6_
  62.4 71.0 %finish_prefix.1 = bf16[1024,896]{1,0:T(8,128)(2,1)S(1)} custom-call(bf16[2,12,256,128]{3,2,1,0:T(8,128)(2,1)S(1)} %get-tuple-element.40.q_ref, s32[8,1024]{1,0:T(8,128)S(1)} %get-tuple-element.43.place_ref, f32[2,12,256,128]{3,2,1,0:T(8,128)S(1)} %get-tuple-element.59.sum_ref, f32[2,256,128]{2,1,0:T(8,128)S(1)} %get-tuple-element.60.total_ref, ...), custom_call_target="tpu_custom_call" | custom-call | flops 6000000000 | bytes 8388608 | tf_op jit(solution)/shard_map/finish_prefix/pallas_call | solution.py:503
  133.4 1.3 copy-done.1
  134.7 40.6 %all-to-all-start.1 = ((bf16[128,8,896]{2,1,0:T(8,128)(2,1)}), bf16[128,8,896]{2,1,0:T(8,128)(2,1)S(1)}, u32[]{:S(2)}, u32[]{:S(2)}) async-start(bf16[128,8,896]{2,1,0:T(8,128)(2,1)} %bitcast.23), calls=%async_computation.1 | async-start | bytes 3670016 | tf_op jit(solution)/shard_map/all_to_all | solution.py:567
  175.3 0.2 convert_reduce_fusion
  175.7 0.1 multiply_add_fusion
  175.8 0.1 reshape.329.at_ref
  175.9 0.2 reshape.325
  176.1 0.8 pad.4.q_ref
  176.8 6.9 %suffix.1 = (f32[8,8,16,128]{3,2,1,0:T(8,128)}, f32[8,8,16,128]{3,2,1,0:T(8,128)}) custom-call(s32[8,16]{1,0:T(8,128)} %table_ref.1, s32[8]{0:T(128)} %len_ref.1, bf16[8,8,16,128]{3,2,1,0:T(8,128)(2,1)} %pad.4.q_ref, bf16[128,16,2048]{2,1,0:T(8,128)(2,1)} %pool_ref.1), custom_call_target="tpu_custom_call" | custom-call | flops 1000000000 | bytes 9437184 | tf_op jit(solution)/shard_map/suffix/pallas_call | solution.py:218
  183.8 1.1 reshape.326.so_ref
  184.9 1.1 reshape.327.sl_ref
  186.0 16.4 %all-to-all-done.1 = bf16[128,8,896]{2,1,0:T(8,128)(2,1)S(1)} async-done(((bf16[128,8,896]{2,1,0:T(8,128)(2,1)}), bf16[128,8,896]{2,1,0:T(8,128)(2,1)S(1)}, u32[]{:S(2)}, u32[]{:S(2)}) %all-to-all-start.1) | async-done | bytes 1835040 | tf_op jit(solution)/shard_map/all_to_all | solution.py:567
  202.4 2.2 %merge.1 = bf16[8,12288]{1,0:T(8,128)(2,1)} custom-call(s32[256,1]{1,0:T(8,128)S(1)} %reshape.329.at_ref, bf16[1024,896]{1,0:T(8,128)(2,1)S(1)} %bitcast.21, f32[8,12288]{1,0:T(8,128)S(1)} %reshape.326.so_ref, f32[8,12288]{1,0:T(8,128)S(1)} %reshape.327.sl_ref), custom_call_target="tpu_custom_call" | custom-call | tf_op jit(solution)/shard_map/merge/pallas_call | solution.py:557
  (19 shorter events, 0.2 us)
Async XLA Ops:
  2.6 35.6 %all-to-all-start = ((bf16[128,8,768]{2,1,0:T(8,128)(2,1)}), bf16[128,8,768]{2,1,0:T(8,128)(2,1)S(1)}, u32[]{:S(2)}, u32[]{:S(2)}) async-start(bf16[128,8,768]{2,1,0:T(8,128)(2,1)} %bitcast.24), calls=%async_computation | async-start | bytes 3145728 | tf_op jit(solution)/shard_map/all_to_all | solution.py:567
  13.8 2.2 %copy-start = (bf16[1,1024,2048]{2,1,0:T(8,128)(2,1)S(1)}, bf16[1,1024,2048]{2,1,0:T(8,128)(2,1)}, u32[]{:S(2)}) copy-start(bf16[1,1024,2048]{2,1,0:T(8,128)(2,1)} %kv_ref.1) | copy-start | bytes 12582916
  19.3 0.8 copy-start.2
  20.1 6.1 %collective-permute-start = (bf16[2,1024,128]{2,1,0:T(8,128)(2,1)S(1)}, bf16[2,1024,128]{2,1,0:T(8,128)(2,1)S(1)}, u32[]{:S(2)}, u32[]{:S(2)}) collective-permute-start(bf16[2,1024,128]{2,1,0:T(8,128)(2,1)S(1)} %get-tuple-element.38), channel_id=1, source_target_pairs={{0,16},{1,17},{2,18},{3,19},{4,20},{5,21},{6,22},{7,23},{8,24},{9,... | collective-permute-start | bytes 1572872 | tf_op jit(solution)/shard_map/ppermute | solution.py:590
  20.1 26.4 %collective-permute-start.1 = (bf16[2,1024,128]{2,1,0:T(8,128)(2,1)}, bf16[2,1024,128]{2,1,0:T(8,128)(2,1)}, u32[]{:S(2)}, u32[]{:S(2)}) collective-permute-start(bf16[2,1024,128]{2,1,0:T(8,128)(2,1)} %get-tuple-element.48), channel_id=1, source_target_pairs={{0,4},{1,5},{2,6},{3,7},{4,8},{5,9},{6,10},{7,11},{8,12},{9,13},{1... | collective-permute-start | bytes 1572872 | tf_op jit(solution)/shard_map/ppermute | solution.py:590
  21.4 25.2 %collective-permute-start.2 = (bf16[2,1024,128]{2,1,0:T(8,128)(2,1)}, bf16[2,1024,128]{2,1,0:T(8,128)(2,1)}, u32[]{:S(2)}, u32[]{:S(2)}) collective-permute-start(bf16[2,1024,128]{2,1,0:T(8,128)(2,1)} %get-tuple-element.49), channel_id=1, source_target_pairs={{0,17},{1,18},{2,19},{3,16},{4,21},{5,22},{6,23},{7,20},{8,25},{9,... | collective-permute-start | bytes 1572872 | tf_op jit(solution)/shard_map/ppermute | solution.py:590
  22.4 24.2 %collective-permute-start.3 = (bf16[2,1024,128]{2,1,0:T(8,128)(2,1)}, bf16[2,1024,128]{2,1,0:T(8,128)(2,1)}, u32[]{:S(2)}, u32[]{:S(2)}) collective-permute-start(bf16[2,1024,128]{2,1,0:T(8,128)(2,1)} %get-tuple-element.50), channel_id=1, source_target_pairs={{0,12},{1,13},{2,14},{3,15},{4,0},{5,1},{6,2},{7,3},{8,4},{9,5},{1... | collective-permute-start | bytes 1572872 | tf_op jit(solution)/shard_map/ppermute | solution.py:590
  25.9 20.7 %collective-permute-start.4 = (bf16[2,1024,128]{2,1,0:T(8,128)(2,1)}, bf16[2,1024,128]{2,1,0:T(8,128)(2,1)}, u32[]{:S(2)}, u32[]{:S(2)}) collective-permute-start(bf16[2,1024,128]{2,1,0:T(8,128)(2,1)} %get-tuple-element.51), channel_id=1, source_target_pairs={{0,19},{1,16},{2,17},{3,18},{4,23},{5,20},{6,21},{7,22},{8,27},{9,... | collective-permute-start | bytes 1572872 | tf_op jit(solution)/shard_map/ppermute | solution.py:590
  40.7 5.9 %copy-start.3 = (bf16[2,1024,128]{2,1,0:T(8,128)(2,1)S(1)}, bf16[2,1024,128]{2,1,0:T(8,128)(2,1)}, u32[]{:S(2)}) copy-start(bf16[2,1024,128]{2,1,0:T(8,128)(2,1)} %copy-done.2) | copy-start | bytes 1572868
  46.6 15.2 %collective-permute-start.6 = (bf16[2,1024,128]{2,1,0:T(8,128)(2,1)S(1)}, bf16[2,1024,128]{2,1,0:T(8,128)(2,1)S(1)}, u32[]{:S(2)}, u32[]{:S(2)}) collective-permute-start(bf16[2,1024,128]{2,1,0:T(8,128)(2,1)S(1)} %copy-done.3), channel_id=1, source_target_pairs={{0,18},{1,19},{2,16},{3,17},{4,22},{5,23},{6,20},{7,21},{8,26},{9,... | collective-permute-start | bytes 1572872 | tf_op jit(solution)/shard_map/ppermute | solution.py:590
  46.7 15.7 %collective-permute-start.5 = (bf16[2,1024,128]{2,1,0:T(8,128)(2,1)S(1)}, bf16[2,1024,128]{2,1,0:T(8,128)(2,1)S(1)}, u32[]{:S(2)}, u32[]{:S(2)}) collective-permute-start(bf16[2,1024,128]{2,1,0:T(8,128)(2,1)S(1)} %get-tuple-element.61), channel_id=1, source_target_pairs={{0,8},{1,9},{2,10},{3,11},{4,12},{5,13},{6,14},{7,15},{8,0},{9,1},... | collective-permute-start | bytes 1572872 | tf_op jit(solution)/shard_map/ppermute | solution.py:590
  133.4 1.3 copy-start.1
  134.7 40.6 %copy-start.5 = (s32[8,1]{0,1:T(1,128)S(1)}, s32[8,1]{0,1:T(1,128)}, u32[]{:S(2)}) copy-start(s32[8,1]{0,1:T(1,128)} %param.7) | copy-start | bytes 100
  134.7 41.2 %copy-start.4 = (bf16[8,12288]{1,0:T(8,128)(2,1)S(1)}, bf16[8,12288]{1,0:T(8,128)(2,1)}, u32[]{:S(2)}) copy-start(bf16[8,12288]{1,0:T(8,128)(2,1)} %q_ref.1) | copy-start | bytes 589828
  134.7 67.7 %all-to-all-start.1 = ((bf16[128,8,896]{2,1,0:T(8,128)(2,1)}), bf16[128,8,896]{2,1,0:T(8,128)(2,1)S(1)}, u32[]{:S(2)}, u32[]{:S(2)}) async-start(bf16[128,8,896]{2,1,0:T(8,128)(2,1)} %bitcast.23), calls=%async_computation.1 | async-start | bytes 3670016 | tf_op jit(solution)/shard_map/all_to_all | solution.py:567

commit v2 on v1

--- a/solution.py
+++ b/solution.py
@@ -26,6 +26,7 @@
 PER_HALF = GROUP // HALVES
 PAIRS = PER_HALF // 2
 PART = PER_HALF * HD
+THIRD = PAIRS * HD
 LINES = HALVES * SLOTS
 ARR = DEVS * LINES
 HALF = DEVS * CAP
@@ -224,7 +225,7 @@
             pltpu.VMEM((ROWS, SPAN, 2 * KVW), BF16),
             pltpu.SemaphoreType.DMA((ROWS,)),
         ],
-        compiler_params=pltpu.CompilerParams(vmem_limit_bytes=56 * MB),
+        compiler_params=pltpu.CompilerParams(vmem_limit_bytes=48 * MB),
         cost_estimate=pl.CostEstimate(
             flops=10**9, bytes_accessed=9 * MB, transcendentals=0
         ),
@@ -382,27 +383,38 @@
     )(rows, place, *kv, *state)
 
 
-def last_kernel(q_ref, place_ref, sum_ref, total_ref, *refs):
-    kv_refs, all_refs, (out_ref, os, ls, ks, vs, sems, held, held_sem) = (
-        refs[:2],
-        refs[2:10],
-        refs[10:],
-    )
+def last_kernel(half, q_ref, place_ref, sum_ref, total_ref, *refs):
+    if half == 0:
+        kv_refs, all_refs, (out_ref, ls, os, ks, vs, sems, held, held_sem) = (
+            refs[:2],
+            refs[2:10],
+            refs[10:],
+        )
+    else:
+        earlier_ls, kv_refs, all_refs, (out_ref, os, ks, vs, sems, held, held_sem, ls) = (
+            refs[0],
+            refs[1:3],
+            refs[3:11],
+            refs[11:],
+        )
     copies = load_blocks(kv_refs, ks, vs, sems)
-    os[...] = jnp.zeros((2, GROUP // 2, HALF, 2 * HD), BF16)
+    os[...] = jnp.zeros((2, HALVES, HALF, THIRD), BF16)
     ls[...] = jnp.zeros((2, HALF, HD), BF16)
     for copy in copies:
         copy.wait()
     lane = iota((TILE, HD), 1)
+    pairs = range(half * PAIRS, (half + 1) * PAIRS)
+    mine = (lane < 3 * GROUP) & (lane % GROUP // PER_HALF == half)
 
     def keep(turn, pair, at, out, totals):
         for i in range(2):
-            os[turn, pair, pl.ds(at, TILE), i * HD : (i + 1) * HD] = (
+            line, column = divmod(2 * pair + i - half * PER_HALF, PAIRS)
+            os[turn, line, pl.ds(at, TILE), column * HD : (column + 1) * HD] = (
                 out[i * TILE : (i + 1) * TILE] / totals[i]
             ).astype(BF16)
 
     def keep_lse(turn, at, total, shift):
-        lse = jnp.where(lane < 3 * GROUP, shift + jnp.log(total), 0.0)
+        lse = jnp.where(mine, shift + jnp.log(total), 0.0)
         one = lse.astype(BF16).astype(F32)
         two = (lse - one).astype(BF16).astype(F32)
         three = lse - one - two
@@ -420,34 +432,30 @@
 
     def step(turn, at):
         before = total_ref[turn, pl.ds(at, TILE), :]
-
-        def one(pair, wide):
+        wide = before
+        for pair in pairs:
             q = pair_rows(q_ref, turn, pair, at)
             out, total = plain_part(q, ks[turn], vs[turn])
             out = out + sum_ref[turn, pl.ds(2 * pair, 2), pl.ds(at, TILE), :].reshape(
                 2 * TILE, HD
             )
             totals = [
-                total[i * TILE : (i + 1) * TILE]
-                + jnp.sum(
-                    jnp.where(lane == 2 * pair + i, before, 0.0), axis=1, keepdims=True
-                )
+                total[i * TILE : (i + 1) * TILE] + before[:, 2 * pair + i : 2 * pair + i + 1]
                 for i in range(2)
             ]
             keep(turn, pair, at, out, totals)
-            return wide + widen(pair, total)
-
-        total = lax.fori_loop(0, GROUP // 2, one, before, unroll=UNROLL)
-        keep_lse(turn, at, total, 0.0)
-        known = jnp.where(lane < 3 * GROUP, total, 1.0)
+            wide = wide + widen(pair, total)
+        keep_lse(turn, at, wide, 0.0)
+        known = jnp.where(mine, wide, 1.0)
         plain = (jnp.min(known) > LEAST) & (jnp.max(known) < MOST)
 
         @pl.when(jnp.logical_not(plain))
         def _():
-            def again(pair, carry):
+            amounts = shifts = jnp.zeros((TILE, HD), F32)
+            for pair in pairs:
                 q = pair_rows(q_ref, turn, pair, at)
 
-                def block(k, state):
+                def block(k, state, q=q):
                     top, amount, acc = state
                     fetch(k, turn)
                     score = dot_t(q, held[0])
@@ -468,11 +476,9 @@
                     ),
                 )
                 keep(turn, pair, at, acc, [amount[:TILE], amount[TILE:]])
-                return carry[0] + widen(pair, amount), carry[1] + widen(pair, top * SCALE)
-
-            empty = jnp.zeros((TILE, HD), F32)
-            amount, shift = lax.fori_loop(0, GROUP // 2, again, (empty, empty))
-            keep_lse(turn, at, amount, shift)
+                amounts = amounts + widen(pair, amount)
+                shifts = shifts + widen(pair, top * SCALE)
+            keep_lse(turn, at, amounts, shifts)
 
     over_tiles(place_ref, step)
 
@@ -481,59 +487,69 @@
     scatter = jnp.concatenate(
         [
             (
-                jnp.where((line_turn(line) == turn) & (line_half(line) == half), place_col, -1)
+                jnp.where((line_turn(line) == turn) & (line_half(line) == part), place_col, -1)
                 == iota((ARR, HALF), 1)
             ).astype(BF16)
             for turn in range(2)
-            for half in range(HALVES)
+            for part in range(HALVES)
         ],
         axis=1,
     )
-    for p in range(PAIRS):
-        source = jnp.concatenate(
-            [os[turn, half * PAIRS + p] for turn in range(2) for half in range(HALVES)], axis=0
-        )
-        out_ref[:, p * 2 * HD : (p + 1) * 2 * HD] = dot(scatter, source).astype(BF16)
-    source = jnp.concatenate([ls[0], ls[0], ls[1], ls[1]], axis=0)
-    out_ref[:, PART:] = dot(scatter, source).astype(BF16)
-
-
-def finish_prefix(rows, place, state, last, everything):
+    source = jnp.concatenate(
+        [os[turn, part] for turn in range(2) for part in range(HALVES)], axis=0
+    )
+    out_ref[:, :THIRD] = dot(scatter, source).astype(BF16)
+    if half == 1:
+        both = [ls[turn] + earlier_ls[turn] for turn in range(2)]
+        source = jnp.concatenate([both[0], both[0], both[1], both[1]], axis=0)
+        out_ref[:, THIRD:] = dot(scatter, source).astype(BF16)
+
+
+def finish_prefix(half, rows, place, state, last, everything, earlier=()):
     vmem = pl.BlockSpec(memory_space=pltpu.VMEM)
+    logs = (2, HALF, HD)
+    out_shape = [jax.ShapeDtypeStruct((ARR, THIRD + half * HD), BF16)]
+    scratch = [
+        pltpu.VMEM((2, HALVES, HALF, THIRD), BF16),
+        *block_scratch(1),
+        pltpu.VMEM((2, BLOCK, HD), BF16),
+        pltpu.SemaphoreType.DMA((1,)),
+    ]
+    if half == 0:
+        out_shape.append(jax.ShapeDtypeStruct(logs, BF16))
+    else:
+        scratch.append(pltpu.VMEM(logs, BF16))
     return pl.pallas_call(
-        last_kernel,
-        out_shape=jax.ShapeDtypeStruct((ARR, PART + HD), BF16),
-        in_specs=[vmem] * 4 + [pl.BlockSpec(memory_space=pl.ANY)] * 10,
-        scratch_shapes=[
-            pltpu.VMEM((2, GROUP // 2, HALF, 2 * HD), BF16),
-            pltpu.VMEM((2, HALF, HD), BF16),
-            *block_scratch(1),
-            pltpu.VMEM((2, BLOCK, HD), BF16),
-            pltpu.SemaphoreType.DMA((1,)),
-        ],
-        compiler_params=pltpu.CompilerParams(vmem_limit_bytes=32 * MB),
+        functools.partial(last_kernel, half),
+        out_shape=out_shape,
+        in_specs=[vmem] * (4 + len(earlier)) + [pl.BlockSpec(memory_space=pl.ANY)] * 10,
+        scratch_shapes=scratch,
+        compiler_params=pltpu.CompilerParams(vmem_limit_bytes=28 * MB),
         cost_estimate=pl.CostEstimate(
             flops=6 * 10**9, bytes_accessed=8 * MB, transcendentals=0
         ),
-        name="finish_prefix",
-    )(rows, place, *state, *last, *everything)
-
-
-def merge_kernel(at_ref, back_ref, so_ref, sl_ref, out_ref):
+        name="finish_%d" % half,
+    )(rows, place, *state, *earlier, *last, *everything)
+
+
+def merge_kernel(at_ref, back0_ref, back1_ref, so_ref, sl_ref, out_ref):
     picked = KVH * 4 * ROWS
     line = iota((picked, ARR), 1)
-    first = dot((at_ref[...] == line).astype(BF16), back_ref[...])
-    second = dot((at_ref[...] + SLOTS == line).astype(BF16), back_ref[:, :PART])
+    first = (at_ref[...] == line).astype(BF16)
+    second = (at_ref[...] + SLOTS == line).astype(BF16)
+    pieces = [dot(first, back0_ref[...]), dot(second, back0_ref[...])]
+    ends = dot(first, back1_ref[...])
+    pieces += [ends[:, :THIRD], dot(second, back1_ref[:, :THIRD])]
     spread = (
         (iota((HD, WIDE), 0) % GROUP == iota((HD, WIDE), 1) // HD)
         & (iota((HD, WIDE), 0) < 3 * GROUP)
     ).astype(BF16)
-    lse = dot(first[:, PART:].astype(BF16), spread)
+    lse = dot(ends[:, THIRD:].astype(BF16), spread)
     for h in range(KVH):
         cut = slice(h * WIDE, (h + 1) * WIDE)
         rows = [slice((h * 4 + j) * ROWS, (h * 4 + j + 1) * ROWS) for j in range(4)]
         parts = [
-            (lse[r], jnp.concatenate([first[r, :PART], second[r]], axis=1)) for r in rows
+            (lse[r], jnp.concatenate([piece[r] for piece in pieces], axis=1)) for r in rows
         ]
         parts.append((sl_ref[:, cut], so_ref[:, cut]))
         top = functools.reduce(jnp.maximum, [p[0] for p in parts])
@@ -543,7 +559,7 @@
         out_ref[:, cut] = (acc / total).astype(BF16)
 
 
-def merge(prompt_ids, back, so, sl):
+def merge(prompt_ids, back0, back1, so, sl):
     prompt = prompt_ids[:, 0]
     earlier = jnp.arange(ROWS)[None, :] < jnp.arange(ROWS)[:, None]
     rank = jnp.sum(((prompt[:, None] == prompt[None, :]) & earlier).astype(jnp.int32), axis=1)
@@ -559,7 +575,7 @@
         out_shape=jax.ShapeDtypeStruct((ROWS, KVH * WIDE), BF16),
         compiler_params=pltpu.CompilerParams(vmem_limit_bytes=16 * MB),
         name="merge",
-    )(at.reshape(-1, 1), back, so, sl)
+    )(at.reshape(-1, 1), back0, back1, so, sl)
 
 
 def exchange(array):
@@ -592,7 +608,8 @@
     kv = list(pieces)
     for n in (1, 2, 3, 6, 7):
         kv[n] = move(n, pieces[n])
-    arrived, kv[1] = lax.optimization_barrier((arrived, kv[1]))
+    so, sl = suffix(page_table, suffix_len, queries, suffix_pool)
+    arrived, kv[1], so, sl = lax.optimization_barrier((arrived, kv[1], so, sl))
     rows, place = gather_rows(arrived)
     place, later = lax.optimization_barrier((place, pieces[4]))
     kv[4] = move(4, later)
@@ -602,10 +619,11 @@
     )
     kv[5] = move(5, later)
     state = add_sums(rows, place, kv[2:4] + kv[6:8], state)
-    parts = finish_prefix(rows, place, state, kv[4:6], kv)
-    parts, queries = lax.optimization_barrier((parts, queries))
-    so, sl = suffix(page_table, suffix_len, queries, suffix_pool)
-    return merge(prompt_ids, exchange(parts), so, sl)
+    part, logs = finish_prefix(0, rows, place, state, kv[4:6], kv)
+    back0 = exchange(part)
+    (part,) = finish_prefix(1, rows, place, state, kv[4:6], kv, (logs,))
+    back1 = exchange(part)
+    return merge(prompt_ids, back0, back1, so, sl)
 
 
 def solution(mesh):

time: 207 us -> 230 us (1.11)
  starting transfers between devices: 60.4 us -> 75.7 us
  Pallas kernels: 102 us -> 110 us
  waiting for transfers between devices: 34.2 us -> 27.8 us
  local copies, waits for them, and re-layouts: 7.56 us -> 12.4 us
    all_to_all x2 -> x3, starting transfers between devices: 51.7 us -> 67.9 us  [exchange(): lax.all_to_all(array.reshape(DEVS, LINES, width), AXES, split_axis=0, con...]
    pallas_call x1 -> x2, Pallas kernels: 71 us -> 79.4 us  [finish_prefix(): pl.pallas_call(functools.partial(last_kernel, half), out_shape=out_shape,...]
    unnamed x12 -> x38, local copies, waits for them, and re-layouts: 4.26 us -> 11.8 us
    all_to_all x2 -> x3, waiting for transfers between devices: 28.4 us -> 22.7 us  [exchange(): lax.all_to_all(array.reshape(DEVS, LINES, width), AXES, split_axis=0, con...]
  transfers between devices with their start and end apart: 9 -> 10, of which waited for: 5 -> 4; matrix products, arithmetic and copies ran while one was open for 2% -> 0% of each run, Pallas kernels for 13% -> 29%
where the time goes in v2:
time: 230 us; the launch traced here: 227 us
  Pallas kernels  110 us (48%)
  starting transfers between devices  75.7 us (33%)
  waiting for transfers between devices  27.8 us (12%)
  local copies, waits for them, and re-layouts  12.4 us (5%)
    pallas_call x2, Pallas kernels, finish_prefix(): pl.pallas_call(functools.partial(last_kernel, half), out_shape=out_shape,...  79.4 us
    all_to_all x3, starting transfers between devices, exchange(): lax.all_to_all(array.reshape(DEVS, LINES, width), AXES, split_axis=0, con...  67.9 us
    all_to_all x3, waiting for transfers between devices, exchange(): lax.all_to_all(array.reshape(DEVS, LINES, width), AXES, split_axis=0, con...  22.7 us
    pallas_call x2, Pallas kernels, add_sums(): pl.pallas_call(functools.partial(sums_kernel, blocks, not state), out_sha...  14.4 us
    unnamed x38, local copies, waits for them, and re-layouts  11.8 us
    ppermute x7, starting transfers between devices, move(): return lax.ppermute(piece, AXES, routes(n // 2, n % 2))  7.74 us
    pallas_call x1, Pallas kernels, suffix(): pl.pallas_call(suffix_kernel, out_shape=[shape, shape], in_specs=[smem, s...  5.6 us
    ppermute x7, waiting for transfers between devices, move(): return lax.ppermute(piece, AXES, routes(n // 2, n % 2))  5.08 us
  transfers between devices with their start and end apart: 10, of which 4 were waited for; matrix products, arithmetic and copies ran while one was open for 0% of the time, Pallas kernels for 29%

profile of v2, /device:TPU:0, one launch (start us, length us, event | category | flops | bytes accessed | tf_op | source)
XLA Modules:
  0.0 227.0 jit_solution(7399136292353070275)
XLA Ops:
  0.0 2.6 %fill_sends.1 = bf16[1024,768]{1,0:T(8,128)(2,1)} custom-call(s32[8]{0:T(128)} %bitcast.30, bf16[8,12288]{1,0:T(8,128)(2,1)} %q_ref.1), custom_call_target="tpu_custom_call" | custom-call | tf_op jit(solution)/shard_map/fill_sends/pallas_call | solution.py:165
  2.6 11.1 %all-to-all-start = ((bf16[128,8,768]{2,1,0:T(8,128)(2,1)}), bf16[128,8,768]{2,1,0:T(8,128)(2,1)S(1)}, u32[]{:S(2)}, u32[]{:S(2)}) async-start(bf16[128,8,768]{2,1,0:T(8,128)(2,1)} %bitcast.29), calls=%async_computation | async-start | bytes 3145728 | tf_op jit(solution)/shard_map/all_to_all | solution.py:583
  13.8 2.2 copy-done
  16.0 3.5 %split_heads.1 = (bf16[2,1024,128]{2,1,0:T(8,128)(2,1)S(1)}, bf16[2,1024,128]{2,1,0:T(8,128)(2,1)}, bf16[2,1024,128]{2,1,0:T(8,128)(2,1)}, bf16[2,1024,128]{2,1,...) custom-call(s32[8]{0:T(128)S(1)} %stack.35.head_ref, ...), custom_call_target="tpu_custom_call" | custom-call | tf_op jit(solution)/shard_map/split_heads/pallas_call | solution.py:101
  19.6 0.8 copy-done.6
  20.4 0.8 copy-done.9
  21.1 0.8 copy-done.11
  22.0 1.2 collective-permute-start.1
  23.2 1.0 collective-permute-start.2
  24.2 3.5 %collective-permute-start.3 = (bf16[2,1024,128]{2,1,0:T(8,128)(2,1)}, bf16[2,1024,128]{2,1,0:T(8,128)(2,1)}, u32[]{:S(2)}, u32[]{:S(2)}) collective-permute-start(bf16[2,1024,128]{2,1,0:T(8,128)(2,1)} %get-tuple-element.54), channel_id=1, source_target_pairs={{0,12},{1,13},{2,14},{3,15},{4,0},{5,1},{6,2},{7,3},{8,4},{9,5},{1... | collective-permute-start | bytes 1572872 | tf_op jit(solution)/shard_map/ppermute | solution.py:606
  27.7 0.3 collective-permute-start.4
  28.3 5.6 %suffix.1 = (f32[8,8,16,128]{3,2,1,0:T(8,128)S(1)}, f32[8,8,16,128]{3,2,1,0:T(8,128)S(1)}) custom-call(s32[8,16]{1,0:T(8,128)S(1)} %copy-done.2, s32[8]{0:T(128)S(1)} %copy-done.3, bf16[8,8,16,128]{3,2,1,0:T(8,128)(2,1)S(1)} %pad.4.q_ref, bf16[128,16,2048]{2,1,0:T(8,128)(2,1)} %pool_ref.1), custom_call_target="tpu_custom_call" | custom-call | flops 1000000000 | bytes 9437184 | tf_op jit(solution)/shard_map/suffix/pallas_call | solution.py:219
  34.0 4.2 %all-to-all-done = bf16[128,8,768]{2,1,0:T(8,128)(2,1)S(1)} async-done(((bf16[128,8,768]{2,1,0:T(8,128)(2,1)}), bf16[128,8,768]{2,1,0:T(8,128)(2,1)S(1)}, u32[]{:S(2)}, u32[]{:S(2)}) %all-to-all-start) | async-done | bytes 1572896 | tf_op jit(solution)/shard_map/all_to_all | solution.py:583
  38.3 2.4 %gather_rows.1 = (bf16[2,12,256,128]{3,2,1,0:T(8,128)(2,1)S(1)}, s32[8,1024]{1,0:T(8,128)S(1)}) custom-call(bf16[1024,768]{1,0:T(8,128)(2,1)S(1)} %bitcast.23), custom_call_target="tpu_custom_call" | custom-call | tf_op jit(solution)/shard_map/gather_rows/pallas_call | solution.py:269
  40.7 1.4 copy-done.7
  42.1 5.4 %sums_1.1 = (f32[2,12,256,128]{3,2,1,0:T(8,128)S(1)}, f32[2,256,128]{2,1,0:T(8,128)S(1)}) custom-call(bf16[2,12,256,128]{3,2,1,0:T(8,128)(2,1)S(1)} %get-tuple-element.44.q_ref, s32[8,1024]{1,0:T(8,128)S(1)} %get-tuple-element.47.place_ref, bf16[2,1024,128]{2,1,0:T(8,128)(2,1)S(1)} %copy-done.7, ...), custom_call_target="tpu_custom_call" | custom-call | flops 4000000000 | bytes 8388608 | tf_op jit(solution)/shard_map/sums_1/pallas_call | solution.py:369
  47.6 0.9 collective-permute-start.6
  48.5 0.8 collective-permute-start.5
  49.3 9.0 %sums_2.1 = (f32[2,12,256,128]{3,2,1,0:T(8,128)S(1)}, f32[2,256,128]{2,1,0:T(8,128)S(1)}) custom-call(bf16[2,12,256,128]{3,2,1,0:T(8,128)(2,1)S(1)} %get-tuple-element.44.q_ref, s32[8,1024]{1,0:T(8,128)S(1)} %get-tuple-element.47.place_ref, bf16[2,1024,128]{2,1,0:T(8,128)(2,1)} %collective-permute-done.1.refs_0_.refs_4_.refs_5_, ...), custom_call_target="tpu_custom_call" | custom-call | flops 8000000000 | bytes 8388608 | tf_op jit(solution)/shard_map/sums_2/pallas_call | solution.py:369
  58.3 3.6 %collective-permute-done.6.refs_1_.refs_7_.refs_2_.refs_8_ = bf16[2,1024,128]{2,1,0:T(8,128)(2,1)S(1)} collective-permute-done((bf16[2,1024,128]{2,1,0:T(8,128)(2,1)S(1)}, bf16[2,1024,128]{2,1,0:T(8,128)(2,1)S(1)}, u32[]{:S(2)}, u32[]{:S(2)}) %collective-permute-start.6) | collective-permute-done | bytes 524320 | tf_op jit(solution)/shard_map/ppermute | solution.py:606
  61.9 1.5 collective-permute-done.5.refs_0_.refs_6_.refs_1_.refs_7_
  63.4 40.0 %finish_0.1 = (bf16[1024,384]{1,0:T(8,128)(2,1)}, bf16[2,256,128]{2,1,0:T(8,128)(2,1)S(1)}) custom-call(bf16[2,12,256,128]{3,2,1,0:T(8,128)(2,1)S(1)} %get-tuple-element.44.q_ref, s32[8,1024]{1,0:T(8,128)S(1)} %get-tuple-element.47.place_ref, f32[2,12,256,128]{3,2,1,0:T(8,128)S(1)} %get-tuple-element.63.sum_ref, ...), custom_call_target="tpu_custom_call" | custom-call | flops 6000000000 | bytes 8388608 | tf_op jit(solution)/shard_map/finish_0/pallas_call | solution.py:522
  103.4 0.6 copy-done.15
  104.1 27.7 %all-to-all-start.1 = ((bf16[128,8,384]{2,1,0:T(8,128)(2,1)}), bf16[128,8,384]{2,1,0:T(8,128)(2,1)S(1)}, u32[]{:S(2)}, u32[]{:S(2)}) async-start(bf16[128,8,384]{2,1,0:T(8,128)(2,1)} %bitcast.11), calls=%async_computation.1 | async-start | bytes 1572864 | tf_op jit(solution)/shard_map/all_to_all | solution.py:583
  131.8 1.4 copy-done.5
  133.2 1.9 copy-done.14
  135.1 0.9 copy-done.16
  136.0 39.4 %finish_1.1 = bf16[1024,512]{1,0:T(8,128)(2,1)S(1)} custom-call(bf16[2,12,256,128]{3,2,1,0:T(8,128)(2,1)S(1)} %copy-done.5, s32[8,1024]{1,0:T(8,128)S(1)} %get-tuple-element.47.place_ref, f32[2,12,256,128]{3,2,1,0:T(8,128)S(1)} %copy-done.14, f32[2,256,128]{2,1,0:T(8,128)S(1)} %get-tuple-element.64.total_ref, bf16[2,256,128]{2,1,0:T(8,128)(2,1)S(1)} %copy-done.16, ...), custom_call_target="tpu_custom_call" | custom-call | flops 6000000000 | bytes 8388608 | tf_op jit(solution)/shard_map/finish_1/pallas_call | solution.py:522
  175.4 1.0 copy-done.1
  176.4 29.1 %all-to-all-start.2 = ((bf16[128,8,512]{2,1,0:T(8,128)(2,1)}), bf16[128,8,512]{2,1,0:T(8,128)(2,1)S(1)}, u32[]{:S(2)}, u32[]{:S(2)}) async-start(bf16[128,8,512]{2,1,0:T(8,128)(2,1)} %bitcast.26), calls=%async_computation.2 | async-start | bytes 2097152 | tf_op jit(solution)/shard_map/all_to_all | solution.py:583
  206.0 18.5 %all-to-all-done.2 = bf16[128,8,512]{2,1,0:T(8,128)(2,1)S(1)} async-done(((bf16[128,8,512]{2,1,0:T(8,128)(2,1)}), bf16[128,8,512]{2,1,0:T(8,128)(2,1)S(1)}, u32[]{:S(2)}, u32[]{:S(2)}) %all-to-all-start.2) | async-done | bytes 1048608 | tf_op jit(solution)/shard_map/all_to_all | solution.py:583
  224.5 2.5 %merge.1 = bf16[8,12288]{1,0:T(8,128)(2,1)} custom-call(s32[256,1]{1,0:T(8,128)S(1)} %reshape.337.at_ref, bf16[1024,384]{1,0:T(8,128)(2,1)S(1)} %bitcast.25, bf16[1024,512]{1,0:T(8,128)(2,1)S(1)} %bitcast.24, f32[8,12288]{1,0:T(8,128)S(1)} %reshape.330.so_ref, f32[8,12288]{1,0:T(8,128)S(1)} %reshape.331.sl_ref), custom_call_target="tpu_custom_call" | custom-call | tf_op jit(solution)/shard_map/merge/pallas_call | solution.py:573
  (48 shorter events, 1.0 us)
Async XLA Ops:
  2.6 25.4 %copy-start.17 = (bf16[8,12288]{1,0:T(8,128)(2,1)S(1)}, bf16[8,12288]{1,0:T(8,128)(2,1)}, u32[]{:S(2)}) copy-start(bf16[8,12288]{1,0:T(8,128)(2,1)} %q_ref.1) | copy-start | bytes 589828
  2.6 35.6 %all-to-all-start = ((bf16[128,8,768]{2,1,0:T(8,128)(2,1)}), bf16[128,8,768]{2,1,0:T(8,128)(2,1)S(1)}, u32[]{:S(2)}, u32[]{:S(2)}) async-start(bf16[128,8,768]{2,1,0:T(8,128)(2,1)} %bitcast.29), calls=%async_computation | async-start | bytes 3145728 | tf_op jit(solution)/shard_map/all_to_all | solution.py:583
  13.8 2.2 copy-start
  16.0 12.3 %copy-start.2 = (s32[8,16]{1,0:T(8,128)S(1)}, s32[8,16]{1,0:T(8,128)}, u32[]{:S(2)}) copy-start(s32[8,16]{1,0:T(8,128)} %table_ref.1) | copy-start | bytes 1540
  16.0 12.3 %copy-start.3 = (s32[8]{0:T(128)S(1)}, s32[8]{0:T(128)}, u32[]{:S(2)}) copy-start(s32[8]{0:T(128)} %len_ref.1) | copy-start | bytes 100
  19.6 0.8 copy-start.6
  20.4 0.8 copy-start.9
  21.1 0.8 copy-start.11
  22.0 12.1 %collective-permute-start = (bf16[2,1024,128]{2,1,0:T(8,128)(2,1)}, bf16[2,1024,128]{2,1,0:T(8,128)(2,1)}, u32[]{:S(2)}, u32[]{:S(2)}) collective-permute-start(bf16[2,1024,128]{2,1,0:T(8,128)(2,1)} %get-tuple-element.40), channel_id=1, source_target_pairs={{0,16},{1,17},{2,18},{3,19},{4,20},{5,21},{6,22},{7,23},{8,24},{9,... | collective-permute-start | bytes 1572872 | tf_op jit(solution)/shard_map/ppermute | solution.py:606
  22.0 25.5 %collective-permute-start.1 = (bf16[2,1024,128]{2,1,0:T(8,128)(2,1)}, bf16[2,1024,128]{2,1,0:T(8,128)(2,1)}, u32[]{:S(2)}, u32[]{:S(2)}) collective-permute-start(bf16[2,1024,128]{2,1,0:T(8,128)(2,1)} %get-tuple-element.52), channel_id=1, source_target_pairs={{0,4},{1,5},{2,6},{3,7},{4,8},{5,9},{6,10},{7,11},{8,12},{9,13},{1... | collective-permute-start | bytes 1572872 | tf_op jit(solution)/shard_map/ppermute | solution.py:606
  23.2 24.3 %collective-permute-start.2 = (bf16[2,1024,128]{2,1,0:T(8,128)(2,1)}, bf16[2,1024,128]{2,1,0:T(8,128)(2,1)}, u32[]{:S(2)}, u32[]{:S(2)}) collective-permute-start(bf16[2,1024,128]{2,1,0:T(8,128)(2,1)} %get-tuple-element.53), channel_id=1, source_target_pairs={{0,17},{1,18},{2,19},{3,16},{4,21},{5,22},{6,23},{7,20},{8,25},{9,... | collective-permute-start | bytes 1572872 | tf_op jit(solution)/shard_map/ppermute | solution.py:606
  24.2 23.3 %collective-permute-start.3 = (bf16[2,1024,128]{2,1,0:T(8,128)(2,1)}, bf16[2,1024,128]{2,1,0:T(8,128)(2,1)}, u32[]{:S(2)}, u32[]{:S(2)}) collective-permute-start(bf16[2,1024,128]{2,1,0:T(8,128)(2,1)} %get-tuple-element.54), channel_id=1, source_target_pairs={{0,12},{1,13},{2,14},{3,15},{4,0},{5,1},{6,2},{7,3},{8,4},{9,5},{1... | collective-permute-start | bytes 1572872 | tf_op jit(solution)/shard_map/ppermute | solution.py:606
  27.7 19.8 %collective-permute-start.4 = (bf16[2,1024,128]{2,1,0:T(8,128)(2,1)}, bf16[2,1024,128]{2,1,0:T(8,128)(2,1)}, u32[]{:S(2)}, u32[]{:S(2)}) collective-permute-start(bf16[2,1024,128]{2,1,0:T(8,128)(2,1)} %get-tuple-element.55), channel_id=1, source_target_pairs={{0,19},{1,16},{2,17},{3,18},{4,23},{5,20},{6,21},{7,22},{8,27},{9,... | collective-permute-start | bytes 1572872 | tf_op jit(solution)/shard_map/ppermute | solution.py:606
  40.7 22.7 %copy-start.4 = (bf16[2,12,256,128]{3,2,1,0:T(8,128)(2,1)}, bf16[2,12,256,128]{3,2,1,0:T(8,128)(2,1)S(1)}, u32[]{:S(2)}) copy-start(bf16[2,12,256,128]{3,2,1,0:T(8,128)(2,1)S(1)} %get-tuple-element.44.q_ref) | copy-start | bytes 4718596
  40.7 1.4 copy-start.7
  42.1 5.4 %copy-start.12 = (bf16[2,1024,128]{2,1,0:T(8,128)(2,1)S(1)}, bf16[2,1024,128]{2,1,0:T(8,128)(2,1)}, u32[]{:S(2)}) copy-start(bf16[2,1024,128]{2,1,0:T(8,128)(2,1)} %copy-done.11) | copy-start | bytes 1572868
  42.1 6.3 %copy-start.10 = (bf16[2,1024,128]{2,1,0:T(8,128)(2,1)S(1)}, bf16[2,1024,128]{2,1,0:T(8,128)(2,1)}, u32[]{:S(2)}) copy-start(bf16[2,1024,128]{2,1,0:T(8,128)(2,1)} %copy-done.9) | copy-start | bytes 1572868
  47.6 15.8 %copy-start.8 = (bf16[2,1024,128]{2,1,0:T(8,128)(2,1)S(1)}, bf16[2,1024,128]{2,1,0:T(8,128)(2,1)}, u32[]{:S(2)}) copy-start(bf16[2,1024,128]{2,1,0:T(8,128)(2,1)} %copy-done.6) | copy-start | bytes 1572868
  47.6 14.3 %collective-permute-start.6 = (bf16[2,1024,128]{2,1,0:T(8,128)(2,1)S(1)}, bf16[2,1024,128]{2,1,0:T(8,128)(2,1)S(1)}, u32[]{:S(2)}, u32[]{:S(2)}) collective-permute-start(bf16[2,1024,128]{2,1,0:T(8,128)(2,1)S(1)} %copy-done.12), channel_id=1, source_target_pairs={{0,18},{1,19},{2,16},{3,17},{4,22},{5,23},{6,20},{7,21},{8,26},{9,... | collective-permute-start | bytes 1572872 | tf_op jit(solution)/shard_map/ppermute | solution.py:606
  48.5 14.9 %collective-permute-start.5 = (bf16[2,1024,128]{2,1,0:T(8,128)(2,1)S(1)}, bf16[2,1024,128]{2,1,0:T(8,128)(2,1)S(1)}, u32[]{:S(2)}, u32[]{:S(2)}) collective-permute-start(bf16[2,1024,128]{2,1,0:T(8,128)(2,1)S(1)} %copy-done.10), channel_id=1, source_target_pairs={{0,8},{1,9},{2,10},{3,11},{4,12},{5,13},{6,14},{7,15},{8,0},{9,1},... | collective-permute-start | bytes 1572872 | tf_op jit(solution)/shard_map/ppermute | solution.py:606
  58.3 45.1 %copy-start.13 = (f32[2,12,256,128]{3,2,1,0:T(8,128)}, f32[2,12,256,128]{3,2,1,0:T(8,128)S(1)}, u32[]{:S(2)}) copy-start(f32[2,12,256,128]{3,2,1,0:T(8,128)S(1)} %get-tuple-element.63.sum_ref) | copy-start | bytes 9437188
  103.4 0.7 copy-start.15
  104.1 72.3 %all-to-all-start.1 = ((bf16[128,8,384]{2,1,0:T(8,128)(2,1)}), bf16[128,8,384]{2,1,0:T(8,128)(2,1)S(1)}, u32[]{:S(2)}, u32[]{:S(2)}) async-start(bf16[128,8,384]{2,1,0:T(8,128)(2,1)} %bitcast.11), calls=%async_computation.1 | async-start | bytes 1572864 | tf_op jit(solution)/shard_map/all_to_all | solution.py:583
  131.8 1.4 copy-start.5
  133.2 1.9 copy-start.14
  135.1 0.9 copy-start.16
  136.0 69.5 %copy-start.18 = (s32[8,1]{0,1:T(1,128)S(1)}, s32[8,1]{0,1:T(1,128)}, u32[]{:S(2)}) copy-start(s32[8,1]{0,1:T(1,128)} %param.7) | copy-start | bytes 100
  175.4 1.0 copy-start.1
  176.4 48.2 %all-to-all-start.2 = ((bf16[128,8,512]{2,1,0:T(8,128)(2,1)}), bf16[128,8,512]{2,1,0:T(8,128)(2,1)S(1)}, u32[]{:S(2)}, u32[]{:S(2)}) async-start(bf16[128,8,512]{2,1,0:T(8,128)(2,1)} %bitcast.26), calls=%async_computation.2 | async-start | bytes 2097152 | tf_op jit(solution)/shard_map/all_to_all | solution.py:583

commit v3 on v1

--- a/solution.py
+++ b/solution.py
@@ -247,9 +247,17 @@
 def gather_kernel(x_ref, q_ref, place_ref):
     pick = (iota((8, HD), 1) == 0).astype(BF16)
     held = dot_t(pick, x_ref[:, :HD]) < EMPTY / 2
-    a, b = iota((ARR, ARR), 0), iota((ARR, ARR), 1)
-    before = (a <= b) & (((a ^ b) & (LINES - CAP)) == 0)
-    place = dot(held.astype(BF16), before.astype(BF16)).astype(jnp.int32) - 1
+    own = iota((8, ARR), 1) % LINES // CAP == iota((8, ARR), 0)
+    mine = (held & own).astype(F32)
+    upto = (iota((HALF, HALF), 0) <= iota((HALF, HALF), 1)).astype(BF16)
+    seen = jnp.zeros((8, 1), F32)
+    counts = []
+    for start in range(0, ARR, HALF):
+        block = mine[:, start : start + HALF]
+        counts.append(dot(block.astype(BF16), upto) + seen)
+        seen = seen + jnp.sum(block, axis=1, keepdims=True)
+    counts = jnp.where(own, jnp.concatenate(counts, axis=1), 0.0)
+    place = jnp.sum(counts, axis=0, keepdims=True).astype(jnp.int32) - 1
     place = jnp.where(held, place, -1)
     place_ref[...] = place
     line = iota((1, ARR), 1)
@@ -305,20 +313,31 @@
 
 
 def load_blocks(kv_refs, ks, vs, sems):
-    copies = []
-    for n, ref in enumerate(kv_refs):
-        rows = pl.ds(n // 2 * BLOCK, BLOCK)
-        copies.append(pltpu.make_async_copy(ref.at[0], ks.at[n % 2, rows], sems.at[n, 0]))
-        copies.append(pltpu.make_async_copy(ref.at[1], vs.at[n % 2, rows], sems.at[n, 1]))
-    for copy in copies:
-        copy.start()
+    copies = [[], []]
+    for turn in range(2):
+        for n in range(turn, len(kv_refs), 2):
+            ref, rows = kv_refs[n], pl.ds(n // 2 * BLOCK, BLOCK)
+            for part, to in enumerate((ks, vs)):
+                copies[turn].append(
+                    pltpu.make_async_copy(ref.at[part], to.at[turn, rows], sems.at[n, part])
+                )
+        for copy in copies[turn]:
+            copy.start()
     return copies
 
 
-def over_tiles(place_ref, step):
+def over_tiles(place_ref, copies, step):
     first, second = [(count + TILE - 1) // TILE for count in row_counts(place_ref)]
 
+    def arrive(turn):
+        for copy in copies[turn]:
+            copy.wait()
+
+    arrive(0)
+    pl.when(second == 0)(lambda: arrive(1))
+
     def tile(t, carry):
+        pl.when((t == first) & (second > 0))(lambda: arrive(1))
         turn = (t >= first).astype(jnp.int32)
         step(turn, pl.multiple_of((t - turn * first) * TILE, TILE))
         return carry
@@ -329,8 +348,7 @@
 def sums_kernel(blocks, first, q_ref, place_ref, *refs):
     kv_refs, refs = refs[: 2 * blocks], refs[2 * blocks :]
     out_ref, total_ref, ks, vs, sems = refs[-5:]
-    for copy in load_blocks(kv_refs, ks, vs, sems):
-        copy.wait()
+    copies = load_blocks(kv_refs, ks, vs, sems)
 
     def step(turn, at):
         def one(pair, wide):
@@ -351,7 +369,7 @@
             0, GROUP // 2, one, wide, unroll=UNROLL
         )
 
-    over_tiles(place_ref, step)
+    over_tiles(place_ref, copies, step)
 
 
 def block_scratch(blocks):
@@ -391,8 +409,6 @@
     copies = load_blocks(kv_refs, ks, vs, sems)
     os[...] = jnp.zeros((2, GROUP // 2, HALF, 2 * HD), BF16)
     ls[...] = jnp.zeros((2, HALF, HD), BF16)
-    for copy in copies:
-        copy.wait()
     lane = iota((TILE, HD), 1)
 
     def keep(turn, pair, at, out, totals):
@@ -474,7 +490,7 @@
             amount, shift = lax.fori_loop(0, GROUP // 2, again, (empty, empty))
             keep_lse(turn, at, amount, shift)
 
-    over_tiles(place_ref, step)
+    over_tiles(place_ref, copies, step)
 
     place_col = jnp.transpose(place_ref[...].astype(F32))[:, 0:1].astype(jnp.int32)
     line = iota((ARR, 1), 0)

time: 207 us -> 206 us (level)
  transfers between devices with their start and end apart: 9 -> 9, of which waited for: 5 -> 5; matrix products, arithmetic and copies ran while one was open for 2% -> 2% of each run, Pallas kernels for 13% -> 12%
where the time goes in v3:
time: 206 us; the launch traced here: 204 us
  Pallas kernels  101 us (49%)
  starting transfers between devices  60.4 us (29%)
  waiting for transfers between devices  35.1 us (17%)
  local copies, waits for them, and re-layouts  7.56 us (4%)
    pallas_call x1, Pallas kernels, finish_prefix(): pl.pallas_call(last_kernel, out_shape=jax.ShapeDtypeStruct((ARR, PART + H...  70.9 us
    all_to_all x2, starting transfers between devices, exchange(): lax.all_to_all(array.reshape(DEVS, LINES, width), AXES, split_axis=0, con...  51.7 us
    all_to_all x2, waiting for transfers between devices, exchange(): lax.all_to_all(array.reshape(DEVS, LINES, width), AXES, split_axis=0, con...  28.4 us
    pallas_call x2, Pallas kernels, add_sums(): pl.pallas_call(functools.partial(sums_kernel, blocks, not state), out_sha...  12.8 us
    ppermute x7, starting transfers between devices, move(): return lax.ppermute(piece, AXES, routes(n // 2, n % 2))  8.67 us
    pallas_call x1, Pallas kernels, suffix(): pl.pallas_call(suffix_kernel, out_shape=[shape, shape], in_specs=[smem, s...  6.94 us
    ppermute x7, waiting for transfers between devices, move(): return lax.ppermute(piece, AXES, routes(n // 2, n % 2))  6.66 us
    unnamed x12, local copies, waits for them, and re-layouts  4.26 us
  transfers between devices with their start and end apart: 9, of which 5 were waited for; matrix products, arithmetic and copies ran while one was open for 2% of the time, Pallas kernels for 12%

profile of v3, /device:TPU:0, one launch (start us, length us, event | category | flops | bytes accessed | tf_op | source)
XLA Modules:
  0.0 204.4 jit_solution(16164715331402431753)
XLA Ops:
  0.0 2.5 %fill_sends.1 = bf16[1024,768]{1,0:T(8,128)(2,1)} custom-call(s32[8]{0:T(128)} %bitcast.27, bf16[8,12288]{1,0:T(8,128)(2,1)} %q_ref.1), custom_call_target="tpu_custom_call" | custom-call | tf_op jit(solution)/shard_map/fill_sends/pallas_call | solution.py:164
  2.5 0.1 stack.35.head_ref
  2.6 11.1 %all-to-all-start = ((bf16[128,8,768]{2,1,0:T(8,128)(2,1)}), bf16[128,8,768]{2,1,0:T(8,128)(2,1)S(1)}, u32[]{:S(2)}, u32[]{:S(2)}) async-start(bf16[128,8,768]{2,1,0:T(8,128)(2,1)} %bitcast.24), calls=%async_computation | async-start | bytes 3145728 | tf_op jit(solution)/shard_map/all_to_all | solution.py:583
  13.8 2.2 %copy-done = bf16[1,1024,2048]{2,1,0:T(8,128)(2,1)S(1)} copy-done((bf16[1,1024,2048]{2,1,0:T(8,128)(2,1)S(1)}, bf16[1,1024,2048]{2,1,0:T(8,128)(2,1)}, u32[]{:S(2)}) %copy-start) | copy-done | bytes 4194328
  16.0 3.4 %split_heads.1 = (bf16[2,1024,128]{2,1,0:T(8,128)(2,1)S(1)}, bf16[2,1024,128]{2,1,0:T(8,128)(2,1)S(1)}, bf16[2,1024,128]{2,1,0:T(8,128)(2,1)}, bf16[2,1024,128]{...) custom-call(s32[8]{0:T(128)S(1)} %stack.35.head_ref, ...), custom_call_target="tpu_custom_call" | custom-call | tf_op jit(solution)/shard_map/split_heads/pallas_call | solution.py:100
  19.3 0.8 copy-done.2
  20.1 1.2 collective-permute-start.1
  21.4 1.0 collective-permute-start.2
  22.4 3.5 %collective-permute-start.3 = (bf16[2,1024,128]{2,1,0:T(8,128)(2,1)}, bf16[2,1024,128]{2,1,0:T(8,128)(2,1)}, u32[]{:S(2)}, u32[]{:S(2)}) collective-permute-start(bf16[2,1024,128]{2,1,0:T(8,128)(2,1)} %get-tuple-element.50), channel_id=1, source_target_pairs={{0,12},{1,13},{2,14},{3,15},{4,0},{5,1},{6,2},{7,3},{8,4},{9,5},{1... | collective-permute-start | bytes 1572872 | tf_op jit(solution)/shard_map/ppermute | solution.py:606
  25.9 0.3 collective-permute-start.4
  26.2 12.0 %all-to-all-done = bf16[128,8,768]{2,1,0:T(8,128)(2,1)S(1)} async-done(((bf16[128,8,768]{2,1,0:T(8,128)(2,1)}), bf16[128,8,768]{2,1,0:T(8,128)(2,1)S(1)}, u32[]{:S(2)}, u32[]{:S(2)}) %all-to-all-start) | async-done | bytes 1572896 | tf_op jit(solution)/shard_map/all_to_all | solution.py:583
  38.2 2.0 %gather_rows.1 = (bf16[2,12,256,128]{3,2,1,0:T(8,128)(2,1)S(1)}, s32[8,1024]{1,0:T(8,128)S(1)}) custom-call(bf16[1024,768]{1,0:T(8,128)(2,1)S(1)} %bitcast.22), custom_call_target="tpu_custom_call" | custom-call | tf_op jit(solution)/shard_map/gather_rows/pallas_call | solution.py:276
  40.3 4.3 %sums_1.1 = (f32[2,12,256,128]{3,2,1,0:T(8,128)S(1)}, f32[2,256,128]{2,1,0:T(8,128)S(1)}) custom-call(bf16[2,12,256,128]{3,2,1,0:T(8,128)(2,1)S(1)} %get-tuple-element.40.q_ref, s32[8,1024]{1,0:T(8,128)S(1)} %get-tuple-element.43.place_ref, bf16[2,1024,128]{2,1,0:T(8,128)(2,1)S(1)} %get-tuple-element.44.refs_0_.refs_2_, ...), custom_call_target="tpu_custom_call" | custom-call | flops 4000000000 | bytes 8388608 | tf_op jit(solution)/shard_map/sums_1/pallas_call | solution.py:386
  44.6 2.0 collective-permute-done.1.refs_0_.refs_4_
  46.6 0.1 collective-permute-start.6
  46.7 2.5 %collective-permute-start.5 = (bf16[2,1024,128]{2,1,0:T(8,128)(2,1)S(1)}, bf16[2,1024,128]{2,1,0:T(8,128)(2,1)S(1)}, u32[]{:S(2)}, u32[]{:S(2)}) collective-permute-start(bf16[2,1024,128]{2,1,0:T(8,128)(2,1)S(1)} %get-tuple-element.61), channel_id=1, source_target_pairs={{0,8},{1,9},{2,10},{3,11},{4,12},{5,13},{6,14},{7,15},{8,0},{9,1},... | collective-permute-start | bytes 1572872 | tf_op jit(solution)/shard_map/ppermute | solution.py:606
  49.2 8.5 %sums_2.1 = (f32[2,12,256,128]{3,2,1,0:T(8,128)S(1)}, f32[2,256,128]{2,1,0:T(8,128)S(1)}) custom-call(bf16[2,12,256,128]{3,2,1,0:T(8,128)(2,1)S(1)} %get-tuple-element.40.q_ref, s32[8,1024]{1,0:T(8,128)S(1)} %get-tuple-element.43.place_ref, bf16[2,1024,128]{2,1,0:T(8,128)(2,1)} %collective-permute-done.1.refs_0_.refs_4_, ...), custom_call_target="tpu_custom_call" | custom-call | flops 8000000000 | bytes 8388608 | tf_op jit(solution)/shard_map/sums_2/pallas_call | solution.py:386
  57.7 4.1 %collective-permute-done.6.refs_1_.refs_7_ = bf16[2,1024,128]{2,1,0:T(8,128)(2,1)S(1)} collective-permute-done((bf16[2,1024,128]{2,1,0:T(8,128)(2,1)S(1)}, bf16[2,1024,128]{2,1,0:T(8,128)(2,1)S(1)}, u32[]{:S(2)}, u32[]{:S(2)}) %collective-permute-start.6) | collective-permute-done | bytes 524320 | tf_op jit(solution)/shard_map/ppermute | solution.py:606
  61.8 0.6 collective-permute-done.5.refs_0_.refs_6_
  62.4 70.9 %finish_prefix.1 = bf16[1024,896]{1,0:T(8,128)(2,1)S(1)} custom-call(bf16[2,12,256,128]{3,2,1,0:T(8,128)(2,1)S(1)} %get-tuple-element.40.q_ref, s32[8,1024]{1,0:T(8,128)S(1)} %get-tuple-element.43.place_ref, f32[2,12,256,128]{3,2,1,0:T(8,128)S(1)} %get-tuple-element.59.sum_ref, f32[2,256,128]{2,1,0:T(8,128)S(1)} %get-tuple-element.60.total_ref, ...), custom_call_target="tpu_custom_call" | custom-call | flops 6000000000 | bytes 8388608 | tf_op jit(solution)/shard_map/finish_prefix/pallas_call | solution.py:519
  133.3 1.3 copy-done.1
  134.6 40.6 %all-to-all-start.1 = ((bf16[128,8,896]{2,1,0:T(8,128)(2,1)}), bf16[128,8,896]{2,1,0:T(8,128)(2,1)S(1)}, u32[]{:S(2)}, u32[]{:S(2)}) async-start(bf16[128,8,896]{2,1,0:T(8,128)(2,1)} %bitcast.23), calls=%async_computation.1 | async-start | bytes 3670016 | tf_op jit(solution)/shard_map/all_to_all | solution.py:583
  175.2 0.2 convert_reduce_fusion
  175.5 0.1 multiply_add_fusion
  175.6 0.1 reshape.329.at_ref
  175.7 0.2 reshape.325
  175.9 0.8 pad.4.q_ref
  176.7 6.9 %suffix.1 = (f32[8,8,16,128]{3,2,1,0:T(8,128)}, f32[8,8,16,128]{3,2,1,0:T(8,128)}) custom-call(s32[8,16]{1,0:T(8,128)} %table_ref.1, s32[8]{0:T(128)} %len_ref.1, bf16[8,8,16,128]{3,2,1,0:T(8,128)(2,1)} %pad.4.q_ref, bf16[128,16,2048]{2,1,0:T(8,128)(2,1)} %pool_ref.1), custom_call_target="tpu_custom_call" | custom-call | flops 1000000000 | bytes 9437184 | tf_op jit(solution)/shard_map/suffix/pallas_call | solution.py:218
  183.6 1.1 reshape.326.so_ref
  184.7 1.1 reshape.327.sl_ref
  185.8 16.4 %all-to-all-done.1 = bf16[128,8,896]{2,1,0:T(8,128)(2,1)S(1)} async-done(((bf16[128,8,896]{2,1,0:T(8,128)(2,1)}), bf16[128,8,896]{2,1,0:T(8,128)(2,1)S(1)}, u32[]{:S(2)}, u32[]{:S(2)}) %all-to-all-start.1) | async-done | bytes 1835040 | tf_op jit(solution)/shard_map/all_to_all | solution.py:583
  202.2 2.2 %merge.1 = bf16[8,12288]{1,0:T(8,128)(2,1)} custom-call(s32[256,1]{1,0:T(8,128)S(1)} %reshape.329.at_ref, bf16[1024,896]{1,0:T(8,128)(2,1)S(1)} %bitcast.21, f32[8,12288]{1,0:T(8,128)S(1)} %reshape.326.so_ref, f32[8,12288]{1,0:T(8,128)S(1)} %reshape.327.sl_ref), custom_call_target="tpu_custom_call" | custom-call | tf_op jit(solution)/shard_map/merge/pallas_call | solution.py:573
  (19 shorter events, 0.2 us)
Async XLA Ops:
  2.6 35.6 %all-to-all-start = ((bf16[128,8,768]{2,1,0:T(8,128)(2,1)}), bf16[128,8,768]{2,1,0:T(8,128)(2,1)S(1)}, u32[]{:S(2)}, u32[]{:S(2)}) async-start(bf16[128,8,768]{2,1,0:T(8,128)(2,1)} %bitcast.24), calls=%async_computation | async-start | bytes 3145728 | tf_op jit(solution)/shard_map/all_to_all | solution.py:583
  13.8 2.2 %copy-start = (bf16[1,1024,2048]{2,1,0:T(8,128)(2,1)S(1)}, bf16[1,1024,2048]{2,1,0:T(8,128)(2,1)}, u32[]{:S(2)}) copy-start(bf16[1,1024,2048]{2,1,0:T(8,128)(2,1)} %kv_ref.1) | copy-start | bytes 12582916
  19.3 0.8 copy-start.2
  20.1 6.1 %collective-permute-start = (bf16[2,1024,128]{2,1,0:T(8,128)(2,1)S(1)}, bf16[2,1024,128]{2,1,0:T(8,128)(2,1)S(1)}, u32[]{:S(2)}, u32[]{:S(2)}) collective-permute-start(bf16[2,1024,128]{2,1,0:T(8,128)(2,1)S(1)} %get-tuple-element.38), channel_id=1, source_target_pairs={{0,16},{1,17},{2,18},{3,19},{4,20},{5,21},{6,22},{7,23},{8,24},{9,... | collective-permute-start | bytes 1572872 | tf_op jit(solution)/shard_map/ppermute | solution.py:606
  20.1 26.4 %collective-permute-start.1 = (bf16[2,1024,128]{2,1,0:T(8,128)(2,1)}, bf16[2,1024,128]{2,1,0:T(8,128)(2,1)}, u32[]{:S(2)}, u32[]{:S(2)}) collective-permute-start(bf16[2,1024,128]{2,1,0:T(8,128)(2,1)} %get-tuple-element.48), channel_id=1, source_target_pairs={{0,4},{1,5},{2,6},{3,7},{4,8},{5,9},{6,10},{7,11},{8,12},{9,13},{1... | collective-permute-start | bytes 1572872 | tf_op jit(solution)/shard_map/ppermute | solution.py:606
  21.4 25.2 %collective-permute-start.2 = (bf16[2,1024,128]{2,1,0:T(8,128)(2,1)}, bf16[2,1024,128]{2,1,0:T(8,128)(2,1)}, u32[]{:S(2)}, u32[]{:S(2)}) collective-permute-start(bf16[2,1024,128]{2,1,0:T(8,128)(2,1)} %get-tuple-element.49), channel_id=1, source_target_pairs={{0,17},{1,18},{2,19},{3,16},{4,21},{5,22},{6,23},{7,20},{8,25},{9,... | collective-permute-start | bytes 1572872 | tf_op jit(solution)/shard_map/ppermute | solution.py:606
  22.4 24.2 %collective-permute-start.3 = (bf16[2,1024,128]{2,1,0:T(8,128)(2,1)}, bf16[2,1024,128]{2,1,0:T(8,128)(2,1)}, u32[]{:S(2)}, u32[]{:S(2)}) collective-permute-start(bf16[2,1024,128]{2,1,0:T(8,128)(2,1)} %get-tuple-element.50), channel_id=1, source_target_pairs={{0,12},{1,13},{2,14},{3,15},{4,0},{5,1},{6,2},{7,3},{8,4},{9,5},{1... | collective-permute-start | bytes 1572872 | tf_op jit(solution)/shard_map/ppermute | solution.py:606
  25.9 20.7 %collective-permute-start.4 = (bf16[2,1024,128]{2,1,0:T(8,128)(2,1)}, bf16[2,1024,128]{2,1,0:T(8,128)(2,1)}, u32[]{:S(2)}, u32[]{:S(2)}) collective-permute-start(bf16[2,1024,128]{2,1,0:T(8,128)(2,1)} %get-tuple-element.51), channel_id=1, source_target_pairs={{0,19},{1,16},{2,17},{3,18},{4,23},{5,20},{6,21},{7,22},{8,27},{9,... | collective-permute-start | bytes 1572872 | tf_op jit(solution)/shard_map/ppermute | solution.py:606
  40.3 6.3 %copy-start.3 = (bf16[2,1024,128]{2,1,0:T(8,128)(2,1)S(1)}, bf16[2,1024,128]{2,1,0:T(8,128)(2,1)}, u32[]{:S(2)}) copy-start(bf16[2,1024,128]{2,1,0:T(8,128)(2,1)} %copy-done.2) | copy-start | bytes 1572868
  46.6 15.2 %collective-permute-start.6 = (bf16[2,1024,128]{2,1,0:T(8,128)(2,1)S(1)}, bf16[2,1024,128]{2,1,0:T(8,128)(2,1)S(1)}, u32[]{:S(2)}, u32[]{:S(2)}) collective-permute-start(bf16[2,1024,128]{2,1,0:T(8,128)(2,1)S(1)} %copy-done.3), channel_id=1, source_target_pairs={{0,18},{1,19},{2,16},{3,17},{4,22},{5,23},{6,20},{7,21},{8,26},{9,... | collective-permute-start | bytes 1572872 | tf_op jit(solution)/shard_map/ppermute | solution.py:606
  46.7 15.7 %collective-permute-start.5 = (bf16[2,1024,128]{2,1,0:T(8,128)(2,1)S(1)}, bf16[2,1024,128]{2,1,0:T(8,128)(2,1)S(1)}, u32[]{:S(2)}, u32[]{:S(2)}) collective-permute-start(bf16[2,1024,128]{2,1,0:T(8,128)(2,1)S(1)} %get-tuple-element.61), channel_id=1, source_target_pairs={{0,8},{1,9},{2,10},{3,11},{4,12},{5,13},{6,14},{7,15},{8,0},{9,1},... | collective-permute-start | bytes 1572872 | tf_op jit(solution)/shard_map/ppermute | solution.py:606
  133.3 1.3 copy-start.1
  134.6 40.6 %copy-start.5 = (s32[8,1]{0,1:T(1,128)S(1)}, s32[8,1]{0,1:T(1,128)}, u32[]{:S(2)}) copy-start(s32[8,1]{0,1:T(1,128)} %param.7) | copy-start | bytes 100
  134.6 41.2 %copy-start.4 = (bf16[8,12288]{1,0:T(8,128)(2,1)S(1)}, bf16[8,12288]{1,0:T(8,128)(2,1)}, u32[]{:S(2)}) copy-start(bf16[8,12288]{1,0:T(8,128)(2,1)} %q_ref.1) | copy-start | bytes 589828
  134.6 67.7 %all-to-all-start.1 = ((bf16[128,8,896]{2,1,0:T(8,128)(2,1)}), bf16[128,8,896]{2,1,0:T(8,128)(2,1)S(1)}, u32[]{:S(2)}, u32[]{:S(2)}) async-start(bf16[128,8,896]{2,1,0:T(8,128)(2,1)} %bitcast.23), calls=%async_computation.1 | async-start | bytes 3670016 | tf_op jit(solution)/shard_map/all_to_all | solution.py:583

commit v4 on v3

--- a/solution.py
+++ b/solution.py
@@ -106,7 +106,7 @@
             pltpu.VMEM((n, 2, BLOCK, HD), BF16),
             pltpu.SemaphoreType.DMA((2, n, 2)),
         ],
-        compiler_params=pltpu.CompilerParams(vmem_limit_bytes=8 * MB),
+        compiler_params=pltpu.CompilerParams(vmem_limit_bytes=60 * MB),
         name="split_heads",
     )(heads, prefix_kv)
 

time: 206 us -> 188 us (0.913)
  Pallas kernels: 101 us -> 90.5 us
  starting transfers between devices: 60.4 us -> 54.5 us
    pallas_call x1, Pallas kernels: 70.9 us -> 59.2 us  [finish_prefix(): pl.pallas_call(last_kernel, out_shape=jax.ShapeDtypeStruct((ARR, PART + H...]
    all_to_all x2, starting transfers between devices: 51.7 us -> 45.6 us  [exchange(): lax.all_to_all(array.reshape(DEVS, LINES, width), AXES, split_axis=0, con...]
    unnamed x12 -> x14, local copies, waits for them, and re-layouts: 4.26 us -> 2.32 us
  transfers between devices with their start and end apart: 9 -> 9, of which waited for: 5 -> 5; matrix products, arithmetic and copies ran while one was open for 2% -> 2% of each run, Pallas kernels for 12% -> 14%
where the time goes in v4:
time: 188 us; the launch traced here: 187 us
  Pallas kernels  90.5 us (48%)
  starting transfers between devices  54.5 us (29%)
  waiting for transfers between devices  35.3 us (19%)
  local copies, waits for them, and re-layouts  6.13 us (3%)
    pallas_call x1, Pallas kernels, finish_prefix(): pl.pallas_call(last_kernel, out_shape=jax.ShapeDtypeStruct((ARR, PART + H...  59.2 us
    all_to_all x2, starting transfers between devices, exchange(): lax.all_to_all(array.reshape(DEVS, LINES, width), AXES, split_axis=0, con...  45.6 us
    all_to_all x2, waiting for transfers between devices, exchange(): lax.all_to_all(array.reshape(DEVS, LINES, width), AXES, split_axis=0, con...  29.7 us
    pallas_call x2, Pallas kernels, add_sums(): pl.pallas_call(functools.partial(sums_kernel, blocks, not state), out_sha...  12.7 us
    ppermute x7, starting transfers between devices, move(): return lax.ppermute(piece, AXES, routes(n // 2, n % 2))  8.84 us
    pallas_call x1, Pallas kernels, suffix(): pl.pallas_call(suffix_kernel, out_shape=[shape, shape], in_specs=[smem, s...  6.93 us
    ppermute x7, waiting for transfers between devices, move(): return lax.ppermute(piece, AXES, routes(n // 2, n % 2))  5.54 us
    pallas_call x1, Pallas kernels, split_heads(): pl.pallas_call(split_heads_kernel, out_shape=[jax.ShapeDtypeStruct((2, BL...  4.98 us
  transfers between devices with their start and end apart: 9, of which 5 were waited for; matrix products, arithmetic and copies ran while one was open for 2% of the time, Pallas kernels for 14%

profile of v4, /device:TPU:0, one launch (start us, length us, event | category | flops | bytes accessed | tf_op | source)
XLA Modules:
  0.0 187.1 jit_solution(18442632408334948183)
XLA Ops:
  0.0 2.5 %fill_sends.1 = bf16[1024,768]{1,0:T(8,128)(2,1)} custom-call(s32[8]{0:T(128)} %bitcast.27, bf16[8,12288]{1,0:T(8,128)(2,1)} %q_ref.1), custom_call_target="tpu_custom_call" | custom-call | tf_op jit(solution)/shard_map/fill_sends/pallas_call | solution.py:164
  2.5 0.6 stack.35.head_ref
  3.1 11.1 %all-to-all-start = ((bf16[128,8,768]{2,1,0:T(8,128)(2,1)}), bf16[128,8,768]{2,1,0:T(8,128)(2,1)S(1)}, u32[]{:S(2)}, u32[]{:S(2)}) async-start(bf16[128,8,768]{2,1,0:T(8,128)(2,1)} %bitcast.24), calls=%async_computation | async-start | bytes 3145728 | tf_op jit(solution)/shard_map/all_to_all | solution.py:583
  14.3 5.0 %split_heads.1 = (bf16[2,1024,128]{2,1,0:T(8,128)(2,1)}, bf16[2,1024,128]{2,1,0:T(8,128)(2,1)}, bf16[2,1024,128]{2,1,0:T(8,128)(2,1)}, bf16[2,1024,128]{2,1,0:T(...) custom-call(s32[8]{0:T(128)} %stack.35.head_ref, ...), custom_call_target="tpu_custom_call" | custom-call | tf_op jit(solution)/shard_map/split_heads/pallas_call | solution.py:100
  19.3 0.1 collective-permute-start
  19.4 1.2 collective-permute-start.1
  20.6 1.0 collective-permute-start.2
  21.6 3.5 %collective-permute-start.3 = (bf16[2,1024,128]{2,1,0:T(8,128)(2,1)}, bf16[2,1024,128]{2,1,0:T(8,128)(2,1)}, u32[]{:S(2)}, u32[]{:S(2)}) collective-permute-start(bf16[2,1024,128]{2,1,0:T(8,128)(2,1)} %get-tuple-element.50), channel_id=1, source_target_pairs={{0,12},{1,13},{2,14},{3,15},{4,0},{5,1},{6,2},{7,3},{8,4},{9,5},{1... | collective-permute-start | bytes 1572872 | tf_op jit(solution)/shard_map/ppermute | solution.py:606
  25.1 0.3 collective-permute-start.4
  25.4 13.3 %all-to-all-done = bf16[128,8,768]{2,1,0:T(8,128)(2,1)S(1)} async-done(((bf16[128,8,768]{2,1,0:T(8,128)(2,1)}), bf16[128,8,768]{2,1,0:T(8,128)(2,1)S(1)}, u32[]{:S(2)}, u32[]{:S(2)}) %all-to-all-start) | async-done | bytes 1572896 | tf_op jit(solution)/shard_map/all_to_all | solution.py:583
  38.7 2.0 %gather_rows.1 = (bf16[2,12,256,128]{3,2,1,0:T(8,128)(2,1)S(1)}, s32[8,1024]{1,0:T(8,128)S(1)}) custom-call(bf16[1024,768]{1,0:T(8,128)(2,1)S(1)} %bitcast.22), custom_call_target="tpu_custom_call" | custom-call | tf_op jit(solution)/shard_map/gather_rows/pallas_call | solution.py:276
  40.8 1.0 copy-done.1
  41.9 4.3 %sums_1.1 = (f32[2,12,256,128]{3,2,1,0:T(8,128)S(1)}, f32[2,256,128]{2,1,0:T(8,128)S(1)}) custom-call(bf16[2,12,256,128]{3,2,1,0:T(8,128)(2,1)S(1)} %get-tuple-element.40.q_ref, s32[8,1024]{1,0:T(8,128)S(1)} %get-tuple-element.43.place_ref, bf16[2,1024,128]{2,1,0:T(8,128)(2,1)S(1)} %copy-done.1, bf16[2,1024,128]{2,1,0:T(8,128)(2,1)S(1)} %collective-permute-done.refs_1_.refs_3_), custom_call_target="tpu_custom_call" | custom-call | flops 4000000000 | bytes 8388608 | tf_op jit(solution)/shard_map/sums_1/pallas_call | solution.py:386
  46.1 0.8 collective-permute-done.1.refs_0_.refs_4_
  47.0 0.1 collective-permute-start.6
  47.1 2.6 %collective-permute-start.5 = (bf16[2,1024,128]{2,1,0:T(8,128)(2,1)S(1)}, bf16[2,1024,128]{2,1,0:T(8,128)(2,1)S(1)}, u32[]{:S(2)}, u32[]{:S(2)}) collective-permute-start(bf16[2,1024,128]{2,1,0:T(8,128)(2,1)S(1)} %copy-done.5), channel_id=1, source_target_pairs={{0,8},{1,9},{2,10},{3,11},{4,12},{5,13},{6,14},{7,15},{8,0},{9,1},... | collective-permute-start | bytes 1572872 | tf_op jit(solution)/shard_map/ppermute | solution.py:606
  49.7 8.4 %sums_2.1 = (f32[2,12,256,128]{3,2,1,0:T(8,128)S(1)}, f32[2,256,128]{2,1,0:T(8,128)S(1)}) custom-call(bf16[2,12,256,128]{3,2,1,0:T(8,128)(2,1)S(1)} %get-tuple-element.40.q_ref, s32[8,1024]{1,0:T(8,128)S(1)} %get-tuple-element.43.place_ref, bf16[2,1024,128]{2,1,0:T(8,128)(2,1)S(1)} %collective-permute-done.1.refs_0_.refs_4_, ...), custom_call_target="tpu_custom_call" | custom-call | flops 8000000000 | bytes 8388608 | tf_op jit(solution)/shard_map/sums_2/pallas_call | solution.py:386
  58.1 4.1 %collective-permute-done.6.refs_1_.refs_7_ = bf16[2,1024,128]{2,1,0:T(8,128)(2,1)S(1)} collective-permute-done((bf16[2,1024,128]{2,1,0:T(8,128)(2,1)S(1)}, bf16[2,1024,128]{2,1,0:T(8,128)(2,1)S(1)}, u32[]{:S(2)}, u32[]{:S(2)}) %collective-permute-start.6) | collective-permute-done | bytes 524320 | tf_op jit(solution)/shard_map/ppermute | solution.py:606
  62.2 0.6 collective-permute-done.5.refs_0_.refs_6_
  62.8 59.2 %finish_prefix.1 = bf16[1024,896]{1,0:T(8,128)(2,1)S(1)} custom-call(bf16[2,12,256,128]{3,2,1,0:T(8,128)(2,1)S(1)} %get-tuple-element.40.q_ref, s32[8,1024]{1,0:T(8,128)S(1)} %get-tuple-element.43.place_ref, f32[2,12,256,128]{3,2,1,0:T(8,128)S(1)} %get-tuple-element.59.sum_ref, f32[2,256,128]{2,1,0:T(8,128)S(1)} %get-tuple-element.60.total_ref, ...), custom_call_target="tpu_custom_call" | custom-call | flops 6000000000 | bytes 8388608 | tf_op jit(solution)/shard_map/finish_prefix/pallas_call | solution.py:519
  122.0 1.3 copy-done
  123.3 34.5 %all-to-all-start.1 = ((bf16[128,8,896]{2,1,0:T(8,128)(2,1)}), bf16[128,8,896]{2,1,0:T(8,128)(2,1)S(1)}, u32[]{:S(2)}, u32[]{:S(2)}) async-start(bf16[128,8,896]{2,1,0:T(8,128)(2,1)} %bitcast.23), calls=%async_computation.1 | async-start | bytes 3670016 | tf_op jit(solution)/shard_map/all_to_all | solution.py:583
  157.8 0.2 convert_reduce_fusion
  158.2 0.1 multiply_add_fusion
  158.3 0.1 reshape.329.at_ref
  158.4 0.2 reshape.325
  158.5 0.8 pad.4.q_ref
  159.3 6.9 %suffix.1 = (f32[8,8,16,128]{3,2,1,0:T(8,128)}, f32[8,8,16,128]{3,2,1,0:T(8,128)}) custom-call(s32[8,16]{1,0:T(8,128)} %table_ref.1, s32[8]{0:T(128)} %len_ref.1, bf16[8,8,16,128]{3,2,1,0:T(8,128)(2,1)} %pad.4.q_ref, bf16[128,16,2048]{2,1,0:T(8,128)(2,1)} %pool_ref.1), custom_call_target="tpu_custom_call" | custom-call | flops 1000000000 | bytes 9437184 | tf_op jit(solution)/shard_map/suffix/pallas_call | solution.py:218
  166.2 1.1 reshape.326.so_ref
  167.3 1.1 reshape.327.sl_ref
  168.4 16.4 %all-to-all-done.1 = bf16[128,8,896]{2,1,0:T(8,128)(2,1)S(1)} async-done(((bf16[128,8,896]{2,1,0:T(8,128)(2,1)}), bf16[128,8,896]{2,1,0:T(8,128)(2,1)S(1)}, u32[]{:S(2)}, u32[]{:S(2)}) %all-to-all-start.1) | async-done | bytes 1835040 | tf_op jit(solution)/shard_map/all_to_all | solution.py:583
  184.9 2.2 %merge.1 = bf16[8,12288]{1,0:T(8,128)(2,1)} custom-call(s32[256,1]{1,0:T(8,128)S(1)} %reshape.329.at_ref, bf16[1024,896]{1,0:T(8,128)(2,1)S(1)} %bitcast.21, f32[8,12288]{1,0:T(8,128)S(1)} %reshape.326.so_ref, f32[8,12288]{1,0:T(8,128)S(1)} %reshape.327.sl_ref), custom_call_target="tpu_custom_call" | custom-call | tf_op jit(solution)/shard_map/merge/pallas_call | solution.py:573
  (21 shorter events, 0.2 us)
Async XLA Ops:
  3.1 35.6 %all-to-all-start = ((bf16[128,8,768]{2,1,0:T(8,128)(2,1)}), bf16[128,8,768]{2,1,0:T(8,128)(2,1)S(1)}, u32[]{:S(2)}, u32[]{:S(2)}) async-start(bf16[128,8,768]{2,1,0:T(8,128)(2,1)} %bitcast.24), calls=%async_computation | async-start | bytes 3145728 | tf_op jit(solution)/shard_map/all_to_all | solution.py:583
  19.3 6.2 %collective-permute-start = (bf16[2,1024,128]{2,1,0:T(8,128)(2,1)}, bf16[2,1024,128]{2,1,0:T(8,128)(2,1)S(1)}, u32[]{:S(2)}, u32[]{:S(2)}) collective-permute-start(bf16[2,1024,128]{2,1,0:T(8,128)(2,1)} %get-tuple-element.38), channel_id=1, source_target_pairs={{0,16},{1,17},{2,18},{3,19},{4,20},{5,21},{6,22},{7,23},{8,24},{9,... | collective-permute-start | bytes 1572872 | tf_op jit(solution)/shard_map/ppermute | solution.py:606
  19.4 27.6 %collective-permute-start.1 = (bf16[2,1024,128]{2,1,0:T(8,128)(2,1)}, bf16[2,1024,128]{2,1,0:T(8,128)(2,1)S(1)}, u32[]{:S(2)}, u32[]{:S(2)}) collective-permute-start(bf16[2,1024,128]{2,1,0:T(8,128)(2,1)} %get-tuple-element.48), channel_id=1, source_target_pairs={{0,4},{1,5},{2,6},{3,7},{4,8},{5,9},{6,10},{7,11},{8,12},{9,13},{1... | collective-permute-start | bytes 1572872 | tf_op jit(solution)/shard_map/ppermute | solution.py:606
  20.6 26.4 %collective-permute-start.2 = (bf16[2,1024,128]{2,1,0:T(8,128)(2,1)}, bf16[2,1024,128]{2,1,0:T(8,128)(2,1)S(1)}, u32[]{:S(2)}, u32[]{:S(2)}) collective-permute-start(bf16[2,1024,128]{2,1,0:T(8,128)(2,1)} %get-tuple-element.49), channel_id=1, source_target_pairs={{0,17},{1,18},{2,19},{3,16},{4,21},{5,22},{6,23},{7,20},{8,25},{9,... | collective-permute-start | bytes 1572872 | tf_op jit(solution)/shard_map/ppermute | solution.py:606
  21.6 25.4 %collective-permute-start.3 = (bf16[2,1024,128]{2,1,0:T(8,128)(2,1)}, bf16[2,1024,128]{2,1,0:T(8,128)(2,1)}, u32[]{:S(2)}, u32[]{:S(2)}) collective-permute-start(bf16[2,1024,128]{2,1,0:T(8,128)(2,1)} %get-tuple-element.50), channel_id=1, source_target_pairs={{0,12},{1,13},{2,14},{3,15},{4,0},{5,1},{6,2},{7,3},{8,4},{9,5},{1... | collective-permute-start | bytes 1572872 | tf_op jit(solution)/shard_map/ppermute | solution.py:606
  25.1 21.9 %collective-permute-start.4 = (bf16[2,1024,128]{2,1,0:T(8,128)(2,1)}, bf16[2,1024,128]{2,1,0:T(8,128)(2,1)}, u32[]{:S(2)}, u32[]{:S(2)}) collective-permute-start(bf16[2,1024,128]{2,1,0:T(8,128)(2,1)} %get-tuple-element.51), channel_id=1, source_target_pairs={{0,19},{1,16},{2,17},{3,18},{4,23},{5,20},{6,21},{7,22},{8,27},{9,... | collective-permute-start | bytes 1572872 | tf_op jit(solution)/shard_map/ppermute | solution.py:606
  40.8 1.0 copy-start.1
  41.8 5.2 %copy-start.6 = (bf16[2,1024,128]{2,1,0:T(8,128)(2,1)S(1)}, bf16[2,1024,128]{2,1,0:T(8,128)(2,1)}, u32[]{:S(2)}) copy-start(bf16[2,1024,128]{2,1,0:T(8,128)(2,1)} %get-tuple-element.62) | copy-start | bytes 1572868
  41.8 5.3 %copy-start.5 = (bf16[2,1024,128]{2,1,0:T(8,128)(2,1)S(1)}, bf16[2,1024,128]{2,1,0:T(8,128)(2,1)}, u32[]{:S(2)}) copy-start(bf16[2,1024,128]{2,1,0:T(8,128)(2,1)} %get-tuple-element.61) | copy-start | bytes 1572868
  47.0 15.8 %copy-start.2 = (bf16[2,1024,128]{2,1,0:T(8,128)(2,1)S(1)}, bf16[2,1024,128]{2,1,0:T(8,128)(2,1)}, u32[]{:S(2)}) copy-start(bf16[2,1024,128]{2,1,0:T(8,128)(2,1)} %get-tuple-element.44.refs_0_.refs_2_) | copy-start | bytes 1572868
  47.0 15.2 %collective-permute-start.6 = (bf16[2,1024,128]{2,1,0:T(8,128)(2,1)S(1)}, bf16[2,1024,128]{2,1,0:T(8,128)(2,1)S(1)}, u32[]{:S(2)}, u32[]{:S(2)}) collective-permute-start(bf16[2,1024,128]{2,1,0:T(8,128)(2,1)S(1)} %copy-done.6), channel_id=1, source_target_pairs={{0,18},{1,19},{2,16},{3,17},{4,22},{5,23},{6,20},{7,21},{8,26},{9,... | collective-permute-start | bytes 1572872 | tf_op jit(solution)/shard_map/ppermute | solution.py:606
  47.1 15.7 %collective-permute-start.5 = (bf16[2,1024,128]{2,1,0:T(8,128)(2,1)S(1)}, bf16[2,1024,128]{2,1,0:T(8,128)(2,1)S(1)}, u32[]{:S(2)}, u32[]{:S(2)}) collective-permute-start(bf16[2,1024,128]{2,1,0:T(8,128)(2,1)S(1)} %copy-done.5), channel_id=1, source_target_pairs={{0,8},{1,9},{2,10},{3,11},{4,12},{5,13},{6,14},{7,15},{8,0},{9,1},... | collective-permute-start | bytes 1572872 | tf_op jit(solution)/shard_map/ppermute | solution.py:606
  122.0 1.3 copy-start
  123.3 34.5 %copy-start.4 = (s32[8,1]{0,1:T(1,128)S(1)}, s32[8,1]{0,1:T(1,128)}, u32[]{:S(2)}) copy-start(s32[8,1]{0,1:T(1,128)} %param.7) | copy-start | bytes 100
  123.3 35.1 %copy-start.3 = (bf16[8,12288]{1,0:T(8,128)(2,1)S(1)}, bf16[8,12288]{1,0:T(8,128)(2,1)}, u32[]{:S(2)}) copy-start(bf16[8,12288]{1,0:T(8,128)(2,1)} %q_ref.1) | copy-start | bytes 589828
  123.3 61.6 %all-to-all-start.1 = ((bf16[128,8,896]{2,1,0:T(8,128)(2,1)}), bf16[128,8,896]{2,1,0:T(8,128)(2,1)S(1)}, u32[]{:S(2)}, u32[]{:S(2)}) async-start(bf16[128,8,896]{2,1,0:T(8,128)(2,1)} %bitcast.23), calls=%async_computation.1 | async-start | bytes 3670016 | tf_op jit(solution)/shard_map/all_to_all | solution.py:583
